TPU v7x, 128 devices: a whole 4x4x4 slice. The times are simulated.
128 devices in a mesh: row: 32 (over y, x_hi, z), col: 4 (over x_lo, core).
Axes of the slice: x: 4 (x_hi: 2, x_lo: 2; x = x_hi * 2 + x_lo), y: 4, z: 4, core: 2. Of those that a mesh axis runs over, the one named last changes fastest.
Arguments:
- factor: float32 [1, 16384, 1, 2048], P(None, 'row', None, 'col'), may hold values from -1 to 2, as said below
- adjoint: float32 [1, 16384, 1, 2048], P(None, 'row', None, 'col'), may hold values from -6 to 6
Outputs:
- updated: float32 [1, 16384, 1, 2048], P(None, 'row', None, 'col')
Inputs may be any that keep to these rules, and one draw needn't show every extreme that they name: `factor`: read as the matrix L, the tiles (0, Q - 2) and (1, Q - 1) are lower triangular with diagonal entries between 1 and 2, tile (0, Q - 1) is zero, and every other tile is dense.
All inputs are finite; a program needn't handle non-finite values.
Results may differ from a plain program's by a relative error of at most 0.00011.
Values sent between devices are 32-bit elements; how exact they have to be, the bound alone decides.
No kernel may reach another device: no remote copies, remote signals or barrier semaphores. Data moves between devices by JAX's collectives and lax.ppermute only.
A program may use at most 64 MiB of HBM per device.

v0:
```python
import jax
import jax.numpy as jnp
from jax import lax
from jax.sharding import PartitionSpec as P

PRECISION_MAX = lax.Precision.HIGHEST


def from_root(value, axis, source):
    kept = jnp.where(lax.axis_index(axis) == source, value, 0).astype(value.dtype)
    return lax.psum(kept, axis)


def block_adjoint(diagonal_block, diag_adj):
    product = jnp.dot(diagonal_block.T, diag_adj, precision=PRECISION_MAX)
    lower = jnp.tril(product, -1) + 0.5 * jnp.diag(jnp.diag(product))
    middle = 0.5 * (lower + lower.T)
    halfway = jax.scipy.linalg.solve_triangular(diagonal_block, middle, lower=True, trans=1)
    return jax.scipy.linalg.solve_triangular(diagonal_block, halfway.T, lower=True, trans=1)


def fetch_rows(factor, diag_tile):
    return from_root(factor[0], "row", diag_tile)


def panel_head(factor, adj, row_panel, column_tile, diag_tile):
    rows_here, tile, cols_here, _ = factor.shape
    row_count = lax.axis_size("row")
    col_count = lax.axis_size("col")
    row_index = lax.axis_index("row")
    col_index = lax.axis_index("col")
    tile_rows = jnp.arange(rows_here, dtype=jnp.int32) * row_count + row_index
    tile_cols = jnp.arange(cols_here, dtype=jnp.int32) * col_count + col_index
    slot = column_tile // col_count
    owner = column_tile % col_count
    owned = col_index == owner
    below = tile_rows > diag_tile
    on_diag_row = (row_index == diag_tile) & (jnp.arange(rows_here) == 0)
    left = tile_cols < column_tile
    diagonal_block = jnp.where(
        owned, jnp.tril(row_panel[:, slot, :]), jnp.eye(tile, dtype=jnp.float32)
    )
    column_multiplier = factor[:, :, slot, :]
    col_adjoint = adj[:, :, slot, :]
    stacked = col_adjoint.transpose(2, 0, 1).reshape(tile, rows_here * tile)
    triangular_solution = jax.scipy.linalg.solve_triangular(
        diagonal_block, stacked, lower=True, trans=1
    )
    triangular_solution = triangular_solution.reshape(tile, rows_here, tile).transpose(1, 2, 0)
    triangular_solution = jnp.where(below[:, None, None], triangular_solution, 0.0)
    local_diagonal = jnp.where(row_index == diag_tile, adj[0, :, slot, :], 0.0)
    diagonal_term = local_diagonal - jnp.einsum(
        "qxd,qxn->dn", triangular_solution, column_multiplier, precision=PRECISION_MAX
    )
    diag_adj = jnp.tril(lax.psum(diagonal_term, "row"))
    block_adj = block_adjoint(diagonal_block, diag_adj)
    solved_all, block_all = (
        from_root(triangular_solution, "col", owner),
        from_root(block_adj, "col", owner),
    )
    top_row = row_index == diag_tile
    return (
        triangular_solution,
        block_adj,
        solved_all,
        block_all,
        slot,
        owned,
        below,
        on_diag_row,
        left,
        top_row,
    )


def row_change(factor, row_panel, solved_all, block_all):
    partial_rows = jnp.einsum("tab,taus->bus", solved_all, factor, precision=PRECISION_MAX)
    total = lax.psum(partial_rows, "row")
    return -total - 2.0 * jnp.einsum("ab,bus->aus", block_all, row_panel, precision=PRECISION_MAX)


def apply_rows(adj, below_change, change, below, left, top_row):
    below_mask = below[:, None] & left[None, :]
    fresh = adj - jnp.where(below_mask[:, None, :, None], below_change, 0.0)
    top_mask = top_row & left[None, :, None]
    return fresh.at[0].set(jnp.where(top_mask, fresh[0] + change, fresh[0]))


def place_column(fresh, triangular_solution, block_adj, slot, owned, below, on_diag_row):
    column_now = fresh[:, :, slot, :]
    column_now = jnp.where(
        (owned & below)[:, None, None],
        triangular_solution,
        jnp.where((owned & on_diag_row)[:, None, None], block_adj[None], column_now),
    )
    return fresh.at[:, :, slot, :].set(column_now)


def one_panel(factor, adj, row_panel, column_tile, diag_tile):
    (
        triangular_solution,
        block_adj,
        solved_all,
        block_all,
        slot,
        owned,
        below,
        on_diag_row,
        left,
        top_row,
    ) = panel_head(factor, adj, row_panel, column_tile, diag_tile)
    change = row_change(factor, row_panel, solved_all, block_all)
    below_change = jnp.einsum("tab,bus->taus", solved_all, row_panel, precision=PRECISION_MAX)
    fresh = apply_rows(adj, below_change, change, below, left, top_row)
    return place_column(fresh, triangular_solution, block_adj, slot, owned, below, on_diag_row)


def local(factor, adjoint):
    col_count = lax.axis_size("col")
    tiles = factor.shape[2] * col_count
    panel_one_rows = fetch_rows(factor, 1)
    adj = one_panel(factor, adjoint, panel_one_rows, tiles - 1, 1)
    panel_two_rows = fetch_rows(factor, 0)
    adj = one_panel(factor, adj, panel_two_rows, tiles - 2, 0)
    return adj


def solution(mesh):
    placed = (P(None, "row", None, "col"), P(None, "row", None, "col"))
    return jax.shard_map(
        local, mesh=mesh, in_specs=placed, out_specs=P(None, "row", None, "col"), check_vma=False
    )
```

profile of v0, /device:TPU:1, one launch (start us, length us, event | category | flops | bytes accessed | tf_op | source)
XLA Modules:
  0.0 1430.5 jit_solution(1553186651667056953)
XLA Ops:
  6.5 2.8 select_bitcast_fusion.1
  9.5 1.1 copy-done.17
  11.7 332.3 %all-reduce.10.cloned.1.call-done = f32[512,512]{1,0:T(8,128)} async-done(((f32[512,512]{1,0:T(8,128)}), f32[512,512]{1,0:T(8,128)}) %all-reduce.10.cloned.1.call-update) | async-done | bytes 1048592 | tf_op jit(solution)/shard_map/psum | solution.py:11
  344.0 1.4 fusion.26
  345.4 8.5 while.16
  346.0 1.4 bitcast_dynamic-update-slice_fusion.4
  348.2 1.4 bitcast_dynamic-update-slice_fusion.4
  350.3 1.4 bitcast_dynamic-update-slice_fusion.4
  352.4 1.4 bitcast_dynamic-update-slice_fusion.4
  353.9 39.3 %custom-call.12 = f32[4,128,128]{1,2,0:T(8,128)S(1)} custom-call(f32[4,128,128]{2,1,0:T(8,128)S(1)} %get-tuple-element.92), custom_call_target="InvertDiagBlocksLowerTriangular" | custom-call | tf_op jit(solution)/shard_map/jit(_solve_triangular)/triangular_solve | solution.py:46
  393.2 1.4 fusion.105
  394.6 1.5 convolution_subtract_fusion.13
  396.6 2.0 convolution_subtract_fusion.12
  399.0 2.5 convolution_subtract_fusion.19
  401.9 1.1 fusion.25
  403.1 1.1 copy-done
  404.3 2.8 convolution_subtract_fusion.1
  407.1 60.1 %all-reduce.12.cloned.1.call-done = f32[512,512]{0,1:T(8,128)} async-done(((f32[512,512]{0,1:T(8,128)}), f32[512,512]{0,1:T(8,128)}) %all-reduce.12.cloned.1.call-update) | async-done | bytes 1048592 | tf_op jit(solution)/shard_map/psum | solution.py:11
  467.2 4.1 convolution_bitcast_fusion.1
  472.8 4.1 fusion.10
  476.9 335.0 %all-reduce.22.cloned.1.call-done = (f32[512,512]{1,0:T(8,128)}, f32[512,1,512]{2,0,1:T(8,128)}, f32[512,512]{1,0:T(8,128)}) async-done(((f32[512,512]{1,0:T(8,128)}, f32[512,1,512]{2,0,1:T(8,128)}, f32[512,512]{1,0:T(8,128)}), (f32[512,512]{1,0:T(8,128)}, f32[512,1,512]{2,0,1:T(8,128)}, f32[512,512]{1,0:T(8,128)})) %all-reduce.22.cloned.1.call-update) | async-done | bytes 3145744 | tf_op jit(solution)/shard_map/psum | solution.py:55
  811.9 3.1 fusion.32
  815.0 1.3 copy.19
  816.3 4.5 gather_fusion
  820.8 1.7 fusion.24
  828.5 1.5 convolution_subtract_fusion.17
  831.1 1.1 fusion.70
  833.4 1.1 fusion.31
  835.3 14.4 %while.17 = (s32[]{:T(128)}, f32[512,512]{1,0:T(8,128)}, s32[4,2]{0,1:T(2,128)S(1)}, f32[4,128,128]{2,1,0:T(8,128)}, s32[]{:T(128)}) while((s32[]{:T(128)}, f32[512,512]{1,0:T(8,128)}, s32[4,2]{0,1:T(2,128)S(1)}, f32[4,128,128]{2,1,0:T(8,128)}, s32[]{:T(128)}) %tuple.88), condition=%wide.while_cond.4.clone.2, body=%wide.while_body.4.clone.2.sunk | while | flops 2 | bytes 132705 | solution.py:46
  835.9 2.9 bitcast_dynamic-update-slice_fusion.5
  839.5 3.0 bitcast_dynamic-update-slice_fusion.5
  843.2 3.0 bitcast_dynamic-update-slice_fusion.5
  846.8 2.9 bitcast_dynamic-update-slice_fusion.5
  849.6 40.8 %custom-call.15 = f32[4,128,128]{1,2,0:T(8,128)} custom-call(f32[4,128,128]{2,1,0:T(8,128)} %get-tuple-element.95), custom_call_target="InvertDiagBlocksLowerTriangular" | custom-call | tf_op jit(solution)/shard_map/jit(_solve_triangular)/triangular_solve | solution.py:46
  890.4 5.9 all-reduce.14.cloned.1.call-done
  896.3 5.1 fusion.6
  901.4 1.6 copy.21
  903.9 1.4 fusion.94
  905.7 1.3 convolution_subtract_fusion.7
  907.3 1.4 convolution_subtract_fusion.6
  909.1 1.7 convolution_subtract_fusion.16
  911.9 1.1 fusion.21
  913.4 57.5 %all-reduce.16.cloned.1.call-done = f32[512,512]{0,1:T(8,128)} async-done(((f32[512,512]{0,1:T(8,128)}), f32[512,512]{0,1:T(8,128)}) %all-reduce.16.cloned.1.call-update) | async-done | bytes 1048592 | tf_op jit(solution)/shard_map/psum | solution.py:11
  971.0 4.0 convolution_select_fusion
  975.0 2.6 copy.24
  977.7 3.3 subtract_bitcast_fusion
  980.9 2.6 copy.22
  983.6 4.2 convolution_subtract_fusion
  987.8 2.9 convolution_bitcast_fusion
  990.7 334.7 %all-reduce.20.cloned.1.call-done = (f32[512,512]{1,0:T(8,128)}, f32[512,1,512]{2,0,1:T(8,128)}) async-done(((f32[512,512]{1,0:T(8,128)}, f32[512,1,512]{2,0,1:T(8,128)}), (f32[512,512]{1,0:T(8,128)}, f32[512,1,512]{2,0,1:T(8,128)})) %all-reduce.20.cloned.1.call-update) | async-done | bytes 2097168 | tf_op jit(solution)/shard_map/psum | solution.py:55
  1325.4 3.1 fusion.34
  1328.5 1.3 copy.23
  1329.8 4.7 gather_fusion.1
  1334.5 1.7 fusion.20
  1342.1 1.5 convolution_subtract_fusion.14
  1344.0 1.6 broadcast_select_fusion
  1345.7 1.2 copy-done.3
  1346.8 1.3 copy.25
  1348.2 2.5 copy.27
  1350.7 59.0 %all-reduce.18.cloned.1.call-done = f32[512,512]{1,0:T(8,128)} async-done(((f32[512,512]{1,0:T(8,128)}), f32[512,512]{1,0:T(8,128)}) %all-reduce.18.cloned.1.call-update) | async-done | bytes 1048592 | tf_op jit(solution)/shard_map/psum | solution.py:11
  1409.8 4.7 fusion.8
  1414.5 2.6 copy.26
  1417.1 2.7 fusion.17
  1419.8 3.6 copy.28
  (127 shorter events, 27.8 us)
Async XLA Ops:
  6.5 337.4 %all-reduce.10.cloned.1.call-start = ((), (), s32[]{:S(2)}) async-start(), calls=%async_computation | async-start | bytes 2097152 | tf_op jit(solution)/shard_map/psum | solution.py:11
  9.4 1.2 copy-start.17
  9.4 457.7 %all-reduce.12.cloned.1.call-start = ((), (), s32[]{:S(2)}) async-start(), calls=%async_computation.1 | async-start | bytes 2097152 | tf_op jit(solution)/shard_map/psum | solution.py:11
  353.9 45.1 %copy-start.14 = (f32[512,512]{1,0:T(8,128)}, f32[512,512]{1,0:T(8,128)S(1)}, u32[]{:S(2)}) copy-start(f32[512,512]{1,0:T(8,128)S(1)} %get-tuple-element.236) | copy-start | bytes 3145732
  393.2 8.3 copy-start.26
  396.6 6.5 copy-start.5
  399.0 4.1 copy-start.8
  401.9 1.2 copy-start.20
  403.0 1.2 copy-start
  403.1 408.8 %all-reduce.22.cloned.1.call-start = ((), (), s32[]{:S(2)}) async-start(), calls=%async_computation.6 | async-start | bytes 6291456 | tf_op jit(solution)/shard_map/psum | solution.py:55
  471.3 1.2 copy-start.2
  471.3 1.5 copy-start.16
  471.3 425.0 %all-reduce.14.cloned.1.call-start = ((), (), s32[]{:S(2)}) async-start(), calls=%async_computation.2 | async-start | bytes 2097152 | tf_op jit(solution)/shard_map/psum | solution.py:11
  820.8 1.7 copy-start.27
  820.8 2.1 copy-start.15
  826.1 4.2 copy-start.7
  827.1 3.3 copy-start.12
  828.5 1.9 copy-start.23
  830.4 0.7 copy-start.28
  832.2 1.2 copy-start.1
  832.2 138.8 %all-reduce.16.cloned.1.call-start = ((), (), s32[]{:S(2)}) async-start(), calls=%async_computation.3 | async-start | bytes 2097152 | tf_op jit(solution)/shard_map/psum | solution.py:11
  902.9 1.0 copy-start.4
  903.9 1.4 copy-start.24
  909.1 2.1 copy-start.10
  911.2 0.7 copy-start.21
  913.0 412.4 %all-reduce.20.cloned.1.call-start = ((), (), s32[]{:S(2)}) async-start(), calls=%async_computation.5 | async-start | bytes 4194304 | tf_op jit(solution)/shard_map/psum | solution.py:55
  975.0 2.6 copy-start.6
  975.0 2.6 copy-start.9
  980.9 2.6 copy-start.11
  980.9 2.6 copy-start.22
  983.6 4.2 copy-start.18
  990.6 419.1 %all-reduce.18.cloned.1.call-start = ((), (), s32[]{:S(2)}) async-start(), calls=%async_computation.4 | async-start | bytes 2097152 | tf_op jit(solution)/shard_map/psum | solution.py:11
  1334.5 1.7 copy-start.25
  1334.5 2.1 copy-start.13
  1345.6 1.2 copy-start.3
  1414.5 2.6 copy-start.19
Sparse Core Ops, SparseCore 0:
  9.8 334.0 all-reduce.9
  403.2 63.9 all-reduce.11
  471.5 340.3 all-reduce.21
  832.3 63.9 all-reduce.13
  913.1 57.8 all-reduce.15
  990.8 334.5 all-reduce.19
  1345.8 63.9 all-reduce.17
where the time goes:
time: 1440 us; the launch traced here: 1430 us
  waiting for transfers between devices  1180 us (82%)
  other arithmetic  101 us (7%)
  matrix products  67.7 us (5%)
  local copies, waits for them, and re-layouts  61.3 us (4%)
  between operations  14.4 us (1%)
    psum x2, waiting for transfers between devices, panel_head(): diag_adj = jnp.tril(lax.psum(diagonal_term, 'row'))  670 us
    psum x5, waiting for transfers between devices, from_root(): return lax.psum(kept, axis)  515 us
    another operation x5, other arithmetic, panel_head(): jax.scipy.linalg.solve_triangular(diagonal_block, stacked, lower=True, tr...  82.5 us
  transfers between devices with their start and end apart: 7, of which 7 were waited for; matrix products, arithmetic and copies ran while one was open for 5% of the time, Pallas kernels for 0%

commit v1 on v0

v1 whole, which is shorter than its diff:
```python
import jax
import jax.numpy as jnp
from jax import lax
from jax.sharding import Mesh
from jax.sharding import PartitionSpec as P
from jax.experimental import pallas as pl
from jax.experimental.pallas import tpu as pltpu

N = 512
H = 256
ALL = ("y", "xh", "z", "xl", "core")
PLANE = ("y", "z")
F32 = jnp.float32
BF16 = jnp.bfloat16


def dev(row, column):
    return row * 4 + column


def split(x):
    hi = x.astype(BF16)
    return hi, (x - hi.astype(F32)).astype(BF16)


def as_parts(x):
    return x if isinstance(x, tuple) else split(x)


def mm(a, b, ta=False):
    ah, al = as_parts(a)
    bh, bl = as_parts(b)
    dims = (((0 if ta else 1,), (0,)), ((), ()))

    def dot(u, v):
        return lax.dot_general(u, v, dims, preferred_element_type=F32)

    return dot(ah, bh) + (dot(ah, bl) + dot(al, bh))


def mmx(a, b):
    return jnp.dot(a, b, preferred_element_type=F32, precision=lax.Precision.HIGHEST)


def iotas(n):
    return (
        lax.broadcasted_iota(jnp.int32, (n, n), 0),
        lax.broadcasted_iota(jnp.int32, (n, n), 1),
    )


def tril(x):
    i, j = iotas(x.shape[0])
    return jnp.where(i >= j, x, 0.0)


def sym_half(p):
    i, j = iotas(p.shape[0])
    low = jnp.where(i > j, p, jnp.where(i == j, 0.5 * p, 0.0))
    return 0.5 * (low + low.T)


def inverse_lower(k_ref, out_ref):
    b = 128
    i, j = iotas(b)
    blocks = [k_ref[s * b:(s + 1) * b, s * b:(s + 1) * b] for s in range(4)]
    inv = [jnp.where(i == j, 1.0 / jnp.where(i == j, t, 1.0), 0.0) for t in blocks]
    size = 1
    while size < b:
        off = (i // (2 * size) == j // (2 * size)) & (i // size > j // size)
        part = [jnp.where(off, t, 0.0) for t in blocks]
        half = [mmx(p, x) for p, x in zip(part, inv)]
        inv = [x - mmx(x, h) for x, h in zip(inv, half)]
        size *= 2
    out_ref[...] = jnp.zeros((N, N), F32)
    for s in range(4):
        out_ref[s * b:(s + 1) * b, s * b:(s + 1) * b] = inv[s]
    for s in (0, 2):
        low = k_ref[(s + 1) * b:(s + 2) * b, s * b:(s + 1) * b]
        out_ref[(s + 1) * b:(s + 2) * b, s * b:(s + 1) * b] = -mmx(inv[s + 1], mmx(low, inv[s]))
    top = out_ref[:H, :H]
    bottom = out_ref[H:, H:]
    out_ref[H:, :H] = -mmx(bottom, mmx(k_ref[H:, :H], top))


def call(kernel, outs, *args):
    vm = pl.BlockSpec(memory_space=pltpu.VMEM)
    sm = pl.BlockSpec(memory_space=pltpu.SMEM)
    return pl.pallas_call(
        kernel,
        out_shape=[jax.ShapeDtypeStruct(s, F32) for s in outs],
        in_specs=[sm if a.dtype == jnp.int32 else vm for a in args],
        out_specs=[vm for _ in outs],
        compiler_params=pltpu.CompilerParams(vmem_limit_bytes=48 * 1024 * 1024),
    )(*args)


def k_inverse(k_ref, y_ref, inv_ref, x_ref):
    inverse_lower(k_ref, inv_ref)
    x_ref[...] = mm(inv_ref[...], y_ref[...])


def k_sum_odd(pos_ref, a_ref, asw_ref, l_ref, lsw_ref, out_ref):
    row, core = pos_ref[0], pos_ref[2]
    second = core == 1
    live = row >= 2
    a3 = split(jnp.where(live, jnp.where(second, a_ref[...], asw_ref[...]), 0.0))
    a2 = split(jnp.where(live, jnp.where(second, asw_ref[...], a_ref[...]), 0.0))
    l3 = split(jnp.where(second, l_ref[:, H:], lsw_ref[:, :H]))
    l2 = split(jnp.where(second, lsw_ref[:, H:], l_ref[:, :H]))
    for t, (a, l) in enumerate(((a3, l3), (a3, l2), (a2, l2))):
        out_ref[:, t] = mm(a, l, ta=True).reshape(16, 32, H)


def k_send(pos_ref, a3_ref, a2_ref, l_ref, slice_ref, x_ref, x12_ref, out_ref):
    row, xl, core = pos_ref[0], pos_ref[1], pos_ref[2]
    zero = jnp.zeros((16, 32, N), F32)

    @pl.when(xl == 1)
    def _():
        out_ref[:, 0] = jnp.broadcast_to(slice_ref[0][None], (16, 32, N))
        out_ref[:, 1] = jnp.broadcast_to(slice_ref[1][None], (16, 32, N))

    @pl.when((xl == 0) & (row >= 2))
    def _():
        l = split(l_ref[...])
        out_ref[:, 0] = mm(a3_ref[...], l, ta=True).reshape(16, 32, N)
        out_ref[:, 1] = mm(a2_ref[...], l, ta=True).reshape(16, 32, N)

    @pl.when((xl == 0) & (row < 2))
    def _():
        out_ref[:, 0] = zero
        out_ref[:, 1] = zero

    @pl.when(row == 0)
    def _():
        out_ref[:, 2] = x_ref[...].reshape(16, 32, N)
        out_ref[:, 3] = (-mm(x12_ref[...], x_ref[...])).reshape(16, 32, N)

    @pl.when(row == 1)
    def _():
        keep = (xl == 0) | (core == 1)
        out_ref[:, 2] = zero
        out_ref[:, 3] = jnp.where(keep, x_ref[...], 0.0).reshape(16, 32, N)

    @pl.when(row >= 2)
    def _():
        out_ref[:, 2] = zero
        out_ref[:, 3] = zero


def k_second(k2_ref, i1_ref, l12_ref, i2_ref, x12_ref):
    x12_ref[...] = mm(i1_ref[...], l12_ref[...])
    inverse_lower(k2_ref, i2_ref)


def k_chain_a(t13_ref, a13_ref, i1_ref, k1_ref, sym_ref):
    g = tril(a13_ref[...] - mm(i1_ref[...], t13_ref[...], ta=True))
    sym_ref[...] = sym_half(mm(tril(k1_ref[...]), g, ta=True))


def k_chain_b(t12_ref, a12_ref, i1_ref, sym_ref, x12_ref, ap_ref):
    inner = t12_ref[...] + 2.0 * mm(sym_ref[...], x12_ref[...])
    ap_ref[...] = a12_ref[...] - mm(i1_ref[...], inner, ta=True)


def k_chain_c(t22_ref, t12_ref, a02_ref, x12_ref, ap_ref, l12_ref, i2_ref, k2_ref, sym_ref):
    inner = t22_ref[...] - mm(x12_ref[...], t12_ref[...], ta=True) + mm(ap_ref[...], l12_ref[...], ta=True)
    g = tril(a02_ref[...] - mm(i2_ref[...], inner, ta=True))
    sym_ref[...] = sym_half(mm(tril(k2_ref[...]), g, ta=True))


def k_chain_d(sym1_ref, i1_ref, sym2_ref, i2_ref, e1_ref, e2_ref):
    for s, i, e in ((sym1_ref, i1_ref, e1_ref), (sym2_ref, i2_ref, e2_ref)):
        inv = split(i[...])
        e[...] = mm(inv, mm(s[...], inv), ta=True)


def k_final(pos_ref, a_ref, a3_ref, a2_ref, got_ref, inv_ref, x_ref, x12_ref, sym_ref, ap_ref, l1_ref, e_ref, out_ref):
    row, xl, core = pos_ref[0], pos_ref[1], pos_ref[2]

    @pl.when(row >= 2)
    def _():
        base = jnp.where(xl == 0, a_ref[...], 0.0)
        m3 = got_ref[:, 3].reshape(N, N)
        m2 = got_ref[:, 2].reshape(N, N)
        out_ref[...] = base - mm(a3_ref[...], m3) - mm(a2_ref[...], m2)

    @pl.when((row == 1) & ((xl == 0) | (core == 0)))
    def _():
        m2 = got_ref[:, 2].reshape(N, N)
        out_ref[...] = -mm(ap_ref[...], m2)

    @pl.when((row == 1) & (xl == 0))
    def _():
        inner = got_ref[:, 0].reshape(N, N) + 2.0 * mm(sym_ref[...], x_ref[...])
        out_ref[...] += a_ref[...] - mm(inv_ref[...], inner, ta=True)

    @pl.when((row == 0) & (xl == 0))
    def _():
        inner = (
            got_ref[:, 1].reshape(N, N)
            - mm(x12_ref[...], got_ref[:, 0].reshape(N, N), ta=True)
            + mm(ap_ref[...], l1_ref[...], ta=True)
            + 2.0 * mm(sym_ref[...], x_ref[...])
        )
        out_ref[...] = a_ref[...] - mm(inv_ref[...], inner, ta=True)

    @pl.when((xl == 1) & (((row == 1) & (core == 1)) | ((row == 0) & (core == 0))))
    def _():
        out_ref[...] = e_ref[...]

    @pl.when((xl == 1) & (row == 0) & (core == 1))
    def _():
        out_ref[...] = a_ref[...]


def move(x, pairs):
    return lax.ppermute(x, ALL, pairs)


def exchange_cores(x, rows, columns):
    return move(x, [(dev(r, c), dev(r, c ^ 1)) for r in rows for c in columns])


def halves(x, core):
    return jnp.where(core == 0, x[:H], x[H:])


def join(mine, other, core):
    return jnp.concatenate([jnp.where(core == 0, mine, other), jnp.where(core == 0, other, mine)], 0)


def swap_xh(x):
    return lax.ppermute(x, "xh", [(0, 1), (1, 0)])


def local(factor, adjoint):
    rows = range(32)
    y, xh, z = (lax.axis_index(n) for n in ("y", "xh", "z"))
    xl, core = lax.axis_index("xl"), lax.axis_index("core")
    row = y * 8 + xh * 4 + z
    pos = jnp.stack([row, xl, core]).astype(jnp.int32)
    first, second = core == 0, core == 1
    low = factor.reshape(N, N)
    adj = adjoint.reshape(N, N)

    adj_sw = exchange_cores(adj, rows, (2, 3))
    low_sw = exchange_cores(low, rows, (2, 3))
    k_odd = jnp.where(row == 1, jnp.where(second, low, low_sw), jnp.where(first, low, low_sw))
    to_even = jnp.where(row <= 1, k_odd, adj)
    at_even = move(to_even, [(dev(r, c), dev(r, c - 2)) for r in rows for c in (2, 3)])
    at_even_sw = exchange_cores(at_even, rows, (0, 1))

    sums_odd, = call(k_sum_odd, [(16, 3, 32, H)], pos, adj, adj_sw, low, low_sw)
    got = lax.all_to_all(sums_odd, PLANE, 0, 0, tiled=True)
    part = jnp.sum(got, axis=0)
    part = part + swap_xh(part)
    odd_slice = jnp.stack([
        jnp.concatenate([part[0], part[1]], 1),
        jnp.concatenate([part[2], jnp.zeros((32, H), F32)], 1),
    ])

    eye = jnp.eye(N, dtype=F32)
    k_own = jnp.where(row <= 1, jnp.where(xl == 1, k_odd, at_even), eye)
    unit = ((row == 1) & (xl == 1) & second) | ((row == 0) & (xl == 1) & first)
    empty = (row == 0) & (xl == 1) & second
    right = jnp.where(unit, -eye, jnp.where(empty, 0.0, low))
    inv, x = call(k_inverse, [(N, N), (N, N)], k_own, right)

    from_zero = move(jnp.where(first, low, adj_sw), [(dev(0, 2), dev(1, 2)), (dev(0, 3), dev(1, 3))])
    from_zero_sw = exchange_cores(from_zero, (1,), (2, 3))
    k2 = jnp.where((row == 1) & (xl == 1), jnp.where(first, from_zero, from_zero_sw), eye)
    a02 = jnp.where(first, from_zero_sw, from_zero)
    l12 = jnp.where(first, low, low_sw)
    i2, x12 = call(k_second, [(N, N), (N, N)], k2, inv, l12)

    half = halves(x12, core)
    to_zero = move(half, [(dev(1, 2), dev(0, 0)), (dev(1, 3), dev(0, 1))])
    to_zero_odd = move(half, [(dev(1, 2), dev(0, 2)), (dev(1, 3), dev(0, 3))])
    mine = jnp.where(xl == 0, to_zero, to_zero_odd)
    x12_zero = join(mine, exchange_cores(mine, (0,), (0, 1, 2, 3)), core)
    l1_zero = move(low, [(dev(1, c), dev(0, c)) for c in (0, 1)])

    a3 = jnp.where(xl == 1, jnp.where(second, adj, adj_sw), jnp.where(second, at_even, at_even_sw))
    a2 = jnp.where(xl == 1, jnp.where(second, adj_sw, adj), jnp.where(second, at_even_sw, at_even))
    send, = call(k_send, [(16, 4, 32, N)], pos, a3, a2, low, odd_slice, x, x12_zero)
    got = lax.all_to_all(send, PLANE, 0, 0, tiled=True)
    part = jnp.sum(got, axis=0)
    part = part + swap_xh(part)

    here = got[:, :2]
    there = exchange_cores(here, (1,), (2, 3))
    left = jnp.where(first, here, there).reshape(16, 2, 32, 2, H)
    rite = jnp.where(first, there, here).reshape(16, 2, 32, 2, H)

    def tile(t):
        pick = [v[:, t // 2, :, t % 2, :].reshape(N, H) for v in (left, rite)]
        return jnp.concatenate(pick, 1)

    t13, t12, t22 = tile(0), tile(1), tile(2)
    k1 = jnp.where(second, low, low_sw)
    a13 = jnp.where(second, adj, adj_sw)
    a12 = jnp.where(second, adj_sw, adj)
    sym1, = call(k_chain_a, [(N, N)], t13, a13, inv, k1)
    ap, = call(k_chain_b, [(N, N)], t12, a12, inv, sym1, x12)
    sym2, = call(k_chain_c, [(N, N)], t22, t12, a02, x12, ap, l12, i2, k2)
    e1, e2 = call(k_chain_d, [(N, N), (N, N)], sym1, inv, sym2, i2)

    def to_even_root(v, r):
        got_half = move(halves(v, core), [(dev(1, 2), dev(r, 0)), (dev(1, 3), dev(r, 1))])
        return join(got_half, exchange_cores(got_half, (r,), (0, 1)), core)

    sym1_even = to_even_root(sym1, 1)
    ap_one = to_even_root(ap, 1)
    ap_zero = to_even_root(ap, 0)
    sym2_even = to_even_root(sym2, 0)
    e2_zero = move(e2, [(dev(1, 2), dev(0, 2))])

    got = lax.all_to_all(jnp.broadcast_to(part[None], (16, 4, 32, N)), PLANE, 0, 0, tiled=True)
    sym = jnp.where(row == 1, sym1_even, sym2_even)
    ap_here = jnp.where(xl == 1, ap, jnp.where(row == 1, ap_one, ap_zero))
    e = jnp.where(row == 1, e1, e2_zero)
    out, = call(k_final, [(N, N)], pos, adj, a3, a2, got, inv, x, x12_zero, sym, ap_here, l1_zero, e)
    return out.reshape(adjoint.shape)


def solution(mesh):
    fine = Mesh(mesh.devices.reshape(4, 2, 4, 2, 2), ALL)
    placed = P(None, ("y", "xh", "z"), None, ("xl", "core"))
    return jax.shard_map(
        local, mesh=fine, in_specs=(placed, placed), out_specs=placed, check_vma=False
    )
```

time: 1440 us -> 312 us (0.22)
  waiting for transfers between devices: 1180 us -> 99.4 us
  other arithmetic: 101 us -> 27 us
  matrix products: 67.7 us -> 0 us
  blocking collectives: 0 us -> 53.3 us
  starting transfers between devices: 1.04 us -> 49.4 us
  Pallas kernels: 0 us -> 43.2 us
  local copies, waits for them, and re-layouts: 61.3 us -> 34.8 us
    psum x7 -> x0, waiting for transfers between devices: 1180 us -> none  [the longest x2 670 us: panel_head(): diag_adj = jnp.tril(lax.psum(diagonal_term, 'row'))]
    ppermute x0 -> x22, waiting for transfers between devices: none -> 99.4 us  [the longest x20 92.2 us: move(): return lax.ppermute(x, ALL, pairs)]
    another operation x7 -> x3, other arithmetic: 84.7 us -> 0.1 us  [the longest x1 0.08 us: local(): pos = jnp.stack([row, xl, core]).astype(jnp.int32)]
    all_to_all x0 -> x1, blocking collectives: none -> 53.3 us  [local(): got = lax.all_to_all(send, PLANE, 0, 0, tiled=True)]
    pallas_call x0 -> x9, Pallas kernels: none -> 43.2 us  [call(): pl.pallas_call(kernel, out_shape=[jax.ShapeDtypeStruct(s, F32) for s in o...]
    dot_general x10 -> x0, matrix products: 38.2 us -> none  [the longest x2 9.8 us: row_change(): jnp.einsum('ab,bus->aus', block_all, row_panel, precision=PRECISION_MAX)]
    ppermute x0 -> x22, starting transfers between devices: none -> 35.7 us  [the longest x20 33.5 us: move(): return lax.ppermute(x, ALL, pairs)]
    another operation x42 -> x0, matrix products: 29.6 us -> none  [the longest x14 14.4 us: panel_head(): jax.scipy.linalg.solve_triangular(diagonal_block, stacked, lower=True, tr...]
  transfers between devices with their start and end apart: 7 -> 24, of which waited for: 7 -> 6; matrix products, arithmetic and copies ran while one was open for 5% -> 13% of each run, Pallas kernels for 0% -> 10%
where the time goes in v1:
time: 312 us; the launch traced here: 308 us
  waiting for transfers between devices  99.4 us (32%)
  blocking collectives  53.3 us (17%)
  starting transfers between devices  49.4 us (16%)
  Pallas kernels  43.2 us (14%)
  local copies, waits for them, and re-layouts  34.8 us (11%)
  other arithmetic  27 us (9%)
    ppermute x20, waiting for transfers between devices, move(): return lax.ppermute(x, ALL, pairs)  92.2 us
    all_to_all x1, blocking collectives, local(): got = lax.all_to_all(send, PLANE, 0, 0, tiled=True)  53.3 us
    pallas_call x9, Pallas kernels, call(): pl.pallas_call(kernel, out_shape=[jax.ShapeDtypeStruct(s, F32) for s in o...  43.2 us
    ppermute x20, starting transfers between devices, move(): return lax.ppermute(x, ALL, pairs)  33.5 us
    unnamed x68, local copies, waits for them, and re-layouts  13.7 us
    all_to_all x1, starting transfers between devices, local(): got = lax.all_to_all(sums_odd, PLANE, 0, 0, tiled=True)  8.27 us
    slice x2, local copies, waits for them, and re-layouts, tile(): pick = [v[:, t // 2, :, t % 2, :].reshape(N, H) for v in (left, rite)]  7.61 us
    ppermute x2, waiting for transfers between devices, swap_xh(): return lax.ppermute(x, 'xh', [(0, 1), (1, 0)])  7.13 us
  transfers between devices with their start and end apart: 24, of which 6 were waited for; matrix products, arithmetic and copies ran while one was open for 13% of the time, Pallas kernels for 10%

profile of v1, /device:TPU:1, one launch (start us, length us, event | category | flops | bytes accessed | tf_op | source)
XLA Modules:
  0.0 308.1 jit_solution(6863066065828203087)
XLA Ops:
  0.0 1.4 copy.39
  1.4 0.7 collective-permute-start
  2.2 1.7 collective-permute-start.1
  3.9 1.0 copy-done.15
  4.9 4.5 %broadcast_select_fusion.3 = (f32[512,512]{1,0:T(8,128)S(1)}, f32[512,512]{1,0:T(8,128)}, f32[512,512]{1,0:T(8,128)S(1)}, f32[512,512]{1,0:T(8,128)S(1)}, f32[512,512]{1,0:T(8,128)}) fusion(f32[512,512]{1,0:T(8,128)} %copy-done.15, pred[]{:T(512)S(6)} %eq.21, f32[1,512,1,512]{3,2,1,0:T(1,128)} %param.2, pred[]{:T(512)S(6)} %and.26, pred[]{:T(512)S(6)} %or.3, ...), kind=kLoop, calls=%fused_computation.23 | loop fusion | flops 2621440 | bytes 9437190 | tf_op jit(solution)/shard_map/jit(_where)/select_n | solution.py:271
  9.4 1.3 collective-permute-start.2
  10.7 1.6 collective-permute-start.5
  12.3 28.1 %collective-permute-done.2 = f32[512,512]{1,0:T(8,128)} collective-permute-done((f32[512,512]{1,0:T(8,128)S(1)}, f32[512,512]{1,0:T(8,128)}, u32[]{:S(2)}, u32[]{:S(2)}) %collective-permute-start.2) | collective-permute-done | bytes 1048608 | tf_op jit(solution)/shard_map/ppermute | solution.py:219
  40.4 2.3 collective-permute-start.3
  42.7 1.7 collective-permute-start.6
  44.5 3.0 shard_map.28
  47.5 1.1 copy-done.17
  48.6 8.3 %all-to-all-start = ((f32[16,3,32,256]{3,2,1,0:T(8,128)}), f32[16,3,32,256]{3,2,1,0:T(8,128)}, u32[]{:S(2)}, u32[]{:S(2)}) async-start(f32[16,3,32,256]{3,2,1,0:T(8,128)} %copy-done.17), calls=%async_computation | async-start | bytes 3145728 | tf_op jit(solution)/shard_map/all_to_all | solution.py:256
  56.9 4.7 %select_select_fusion = (f32[512,512]{1,0:T(8,128)S(1)}, f32[512,512]{1,0:T(8,128)}, f32[512,512]{1,0:T(8,128)}, f32[512,512]{1,0:T(8,128)}, f32[512,512]{1,0:T(8,128)S(1)}) fusion(f32[512,512]{1,0:T(8,128)} %collective-permute-done.3, f32[512,512]{1,0:T(8,128)} %collective-permute-done.2, pred[]{:T(512)S(6)} %eq.19, pred[]{:T(512)S(6)} %eq.18, ...), kind=kLoop, calls=%fused_computation.14 | loop fusion | flops 2883584 | bytes 11534340 | tf_op jit(solution)/shard_map/jit(_where)/select_n | solution.py:286
  61.6 6.0 %shard_map.29 = (f32[512,512]{1,0:T(8,128)S(1)}, f32[512,512]{1,0:T(8,128)S(1)}) custom-call(f32[512,512]{1,0:T(8,128)S(1)} %get-tuple-element.51.k_ref, f32[512,512]{1,0:T(8,128)S(1)} %copy-done.24), custom_call_target="tpu_custom_call" | custom-call | tf_op jit(solution)/shard_map/pallas_call | solution.py:89
  67.6 3.1 %broadcast_select_fusion.2 = (f32[512,512]{1,0:T(8,128)}, f32[512,512]{1,0:T(8,128)S(1)}) fusion(f32[512,512]{1,0:T(8,128)} %collective-permute-done.6, f32[512,512]{1,0:T(8,128)} %collective-permute-done.5, pred[]{:T(512)S(6)} %eq.21, pred[]{:T(512)S(6)} %and.22), kind=kLoop, calls=%fused_computation.22 | loop fusion | flops 1310720 | bytes 4194306 | tf_op jit(solution)/shard_map/jit(_where)/select_n | solution.py:274
  70.8 6.6 %shard_map.30 = (f32[512,512]{1,0:T(8,128)S(1)}, f32[512,512]{1,0:T(8,128)S(1)}) custom-call(f32[512,512]{1,0:T(8,128)S(1)} %get-tuple-element.29.k2_ref, f32[512,512]{1,0:T(8,128)S(1)} %get-tuple-element.12.i1_ref.inv_ref, f32[512,512]{1,0:T(8,128)S(1)} %get-tuple-element.49.l12_ref), custom_call_target="tpu_custom_call" | custom-call | tf_op jit(solution)/shard_map/pallas_call | solution.py:89
  77.4 1.0 copy-done.23
  78.5 1.3 collective-permute-start.7
  79.8 1.5 collective-permute-start.8
  81.2 1.5 reduce_sum.18
  82.7 2.1 collective-permute-start.4
  84.8 9.6 %collective-permute-done.7 = f32[256,512]{1,0:T(8,128)S(1)} collective-permute-done((f32[256,512]{1,0:T(8,128)S(1)}, f32[256,512]{1,0:T(8,128)S(1)}, u32[]{:S(2)}, u32[]{:S(2)}) %collective-permute-start.7) | collective-permute-done | bytes 524320 | tf_op jit(solution)/shard_map/ppermute | solution.py:219
  94.5 3.9 %collective-permute-start.9 = (f32[256,512]{1,0:T(8,128)S(1)}, f32[256,512]{1,0:T(8,128)S(1)}, u32[]{:S(2)}, u32[]{:S(2)}) collective-permute-start(f32[256,512]{1,0:T(8,128)S(1)} %broadcast_select_fusion.11), channel_id=1, source_target_pairs={{0,1},{1,0},{2,3},{3,2}} | collective-permute-start | bytes 1572872 | tf_op jit(solution)/shard_map/ppermute | solution.py:219
  98.5 1.4 collective-permute-done.9
  100.4 3.8 %shard_map.31 = f32[16,4,32,512]{3,2,1,0:T(8,128)} custom-call(s32[3]{0:T(128)S(1)} %pad_add_fusion.pos_ref, f32[512,512]{1,0:T(8,128)S(1)} %copy-done.3, f32[512,512]{1,0:T(8,128)S(1)} %get-tuple-element.17.a2_ref, f32[512,512]{1,0:T(8,128)S(1)} %bitcast.53, f32[2,32,512]{2,1,0:T(8,128)S(1)} %pad_maximum_fusion.4.slice_ref, f32[512,512]{1,0:T(8,128)S(1)} %copy-done.19, ...), custom_call_target="tpu_custom_call" | custom-call | tf_op jit(solution)/shard_map/pallas_call | solution.py:89
  104.1 53.3 %all_to_all.15 = f32[16,4,32,512]{3,2,1,0:T(8,128)S(1)} all-to-all(f32[16,4,32,512]{3,2,1,0:T(8,128)} %shard_map.31), channel_id=1, replica_groups=mesh['y'=4,'xh'=2,'z'=4,'xl'=2,'core'=2] {'y','z'}, dimensions={0} | all-to-all | bytes 8388608 | tf_op jit(solution)/shard_map/all_to_all | solution.py:288
  157.4 1.8 slice.77
  159.2 0.9 copy-done.25
  160.1 2.0 collective-permute-start.11
  162.1 2.6 reduce_sum.19
  164.8 7.1 %collective-permute-done.10 = f32[4,32,512]{2,1,0:T(8,128)S(1)} collective-permute-done((f32[4,32,512]{2,1,0:T(8,128)S(1)}, f32[4,32,512]{2,1,0:T(8,128)S(1)}, u32[]{:S(2)}, u32[]{:S(2)}) %collective-permute-start.10) | collective-permute-done | bytes 262176 | tf_op jit(solution)/shard_map/ppermute | solution.py:235
  172.0 2.5 broadcast_in_dim.12
  174.5 5.5 %all-to-all-start.2 = ((f32[16,4,32,512]{3,2,1,0:T(8,128)}), f32[16,4,32,512]{3,2,1,0:T(8,128)}, u32[]{:S(2)}, u32[]{:S(2)}) async-start(f32[16,4,32,512]{3,2,1,0:T(8,128)} %broadcast_in_dim.12), calls=%async_computation.2 | async-start | bytes 8388608 | tf_op jit(solution)/shard_map/all_to_all | solution.py:320
  180.1 5.1 %broadcast_select_fusion.1 = (f32[16,2,32,512]{3,2,1,0:T(8,128)}, f32[16,2,32,512]{3,2,1,0:T(8,128)}) fusion(f32[16,2,32,512]{3,2,1,0:T(8,128)} %collective-permute-done.11, pred[]{:T(512)S(6)} %eq.21, f32[16,4,32,512]{3,2,1,0:T(8,128)} %copy-done.25), kind=kLoop, calls=%fused_computation.17 | loop fusion | flops 1048576 | bytes 8388609 | tf_op jit(solution)/shard_map/jit(_where)/select_n | solution.py:294
  185.2 3.5 %reshape.18 = f32[16,2,32,2,256]{4,3,2,1,0:T(2,128)} reshape(f32[16,2,32,512]{3,2,1,0:T(8,128)} %get-tuple-element.24) | data formatting | bytes 4194304 | tf_op jit(solution)/shard_map/reshape | solution.py:294
  188.7 4.3 %fusion.2 = (f32[16,1,32,1,256]{4,3,2,1,0:T(1,128)S(1)}, f32[16,1,32,1,256]{4,3,2,1,0:T(1,128)}, f32[16,1,32,1,256]{4,3,2,1,0:T(1,128)}) fusion(f32[16,2,32,2,256]{4,3,2,1,0:T(2,128)} %reshape.18), kind=kLoop, calls=%fused_computation.49 | loop fusion | bytes 3145728 | tf_op jit(solution)/shard_map/slice | solution.py:298
  193.0 0.8 copy.16
  193.8 3.7 %reshape.19 = f32[16,2,32,2,256]{4,3,2,1,0:T(2,128)} reshape(f32[16,2,32,512]{3,2,1,0:T(8,128)} %get-tuple-element.25) | data formatting | bytes 4194304 | tf_op jit(solution)/shard_map/reshape | solution.py:295
  197.5 3.4 %fusion.3 = (f32[16,1,32,1,256]{4,3,2,1,0:T(1,128)S(1)}, f32[16,1,32,1,256]{4,3,2,1,0:T(1,128)S(1)}, f32[16,1,32,1,256]{4,3,2,1,0:T(1,128)S(1)}) fusion(f32[16,2,32,2,256]{4,3,2,1,0:T(2,128)} %reshape.19), kind=kLoop, calls=%fused_computation.50 | loop fusion | bytes 3145728 | tf_op jit(solution)/shard_map/slice | solution.py:298
  201.0 0.9 copy-done.28
  202.1 1.0 copy-done.14
  203.4 2.0 shard_map.32.sym_ref.sym1_ref
  205.6 1.1 copy-done.22
  206.7 3.2 %shard_map.33.ap_ref = f32[512,512]{1,0:T(8,128)S(1)} custom-call(f32[512,512]{1,0:T(8,128)S(1)} %pad_maximum_fusion.3.t12_ref, f32[512,512]{1,0:T(8,128)S(1)} %copy-done.22, f32[512,512]{1,0:T(8,128)S(1)} %get-tuple-element.12.i1_ref.inv_ref, f32[512,512]{1,0:T(8,128)S(1)} %shard_map.32.sym_ref.sym1_ref, f32[512,512]{1,0:T(8,128)} %copy-done.11), custom_call_target="tpu_custom_call" | custom-call | tf_op jit(solution)/shard_map/pallas_call | solution.py:89
  209.9 1.0 copy-done
  211.0 1.1 copy-done.12
  212.4 6.0 %shard_map.34.sym2_ref = f32[512,512]{1,0:T(8,128)S(1)} custom-call(f32[512,512]{1,0:T(8,128)S(1)} %pad_maximum_fusion.2.t22_ref, f32[512,512]{1,0:T(8,128)S(1)} %pad_maximum_fusion.3.t12_ref, f32[512,512]{1,0:T(8,128)S(1)} %copy-done.21, f32[512,512]{1,0:T(8,128)S(1)} %copy-done.12, f32[512,512]{1,0:T(8,128)} %copy-done, f32[512,512]{1,0:T(8,128)} %copy-done.2, ...), custom_call_target="tpu_custom_call" | custom-call | tf_op jit(solution)/shard_map/pallas_call | solution.py:89
  218.5 4.9 %shard_map.35 = (f32[512,512]{1,0:T(8,128)S(1)}, f32[512,512]{1,0:T(8,128)S(1)}) custom-call(f32[512,512]{1,0:T(8,128)S(1)} %shard_map.32.sym_ref.sym1_ref, f32[512,512]{1,0:T(8,128)S(1)} %get-tuple-element.12.i1_ref.inv_ref, f32[512,512]{1,0:T(8,128)S(1)} %shard_map.34.sym2_ref, f32[512,512]{1,0:T(8,128)} %copy-done.23), custom_call_target="tpu_custom_call" | custom-call | tf_op jit(solution)/shard_map/pallas_call | solution.py:89
  223.4 0.9 collective-permute-start.21
  224.4 1.3 collective-permute-start.18
  225.7 0.7 collective-permute-start.16
  226.5 1.3 collective-permute-start.14
  228.6 35.6 %collective-permute-done.14 = f32[256,512]{1,0:T(8,128)S(1)} collective-permute-done((f32[256,512]{1,0:T(8,128)S(1)}, f32[256,512]{1,0:T(8,128)S(1)}, u32[]{:S(2)}, u32[]{:S(2)}) %collective-permute-start.14) | collective-permute-done | bytes 524320 | tf_op jit(solution)/shard_map/ppermute | solution.py:219
  264.1 6.0 %collective-permute-start.15 = (f32[256,512]{1,0:T(8,128)S(1)}, f32[256,512]{1,0:T(8,128)S(1)}, u32[]{:S(2)}, u32[]{:S(2)}) collective-permute-start(f32[256,512]{1,0:T(8,128)S(1)} %collective-permute-done.14), channel_id=1, source_target_pairs={{0,1},{1,0}} | collective-permute-start | bytes 1572872 | tf_op jit(solution)/shard_map/ppermute | solution.py:219
  270.1 1.3 collective-permute-start.20
  271.5 2.1 collective-permute-start.19
  275.0 1.2 broadcast_select_fusion.5.e_ref
  276.5 1.2 maximum_select_fusion.sym_ref
  277.9 1.4 fusion.1.ap_ref
  279.3 17.6 %collective-permute-done.20.l1_ref = f32[512,512]{1,0:T(8,128)} collective-permute-done((f32[512,512]{1,0:T(8,128)S(1)}, f32[512,512]{1,0:T(8,128)}, u32[]{:S(2)}, u32[]{:S(2)}) %collective-permute-start.20) | collective-permute-done | bytes 1048608 | tf_op jit(solution)/shard_map/ppermute | solution.py:219
  296.9 1.2 copy-done.7
  298.2 7.7 %shard_map.36 = f32[512,512]{1,0:T(8,128)S(1)} custom-call(s32[3]{0:T(128)S(1)} %pad_add_fusion.pos_ref, f32[512,512]{1,0:T(8,128)S(1)} %bitcast.50, f32[512,512]{1,0:T(8,128)S(1)} %copy-done.3, f32[512,512]{1,0:T(8,128)S(1)} %get-tuple-element.17.a2_ref, f32[16,4,32,512]{3,2,1,0:T(8,128)} %all-to-all-done.2.got_ref, ...), custom_call_target="tpu_custom_call" | custom-call | tf_op jit(solution)/shard_map/pallas_call | solution.py:89
  305.9 2.0 copy.9
  (98 shorter events, 5.1 us)
Async XLA Ops:
  0.0 2.1 copy-start.26
  1.4 43.1 %copy-start.6 = (f32[1,512,1,512]{3,1,2,0:T(8,128)}, f32[1,512,1,512]{3,1,2,0:T(8,128)S(1)}, u32[]{:S(2)}) copy-start(f32[1,512,1,512]{3,1,2,0:T(8,128)S(1)} %copy.39) | copy-start | bytes 3145732
  1.4 2.5 collective-permute-start
  2.2 42.3 %copy-start.8 = (f32[1,512,1,512]{3,1,2,0:T(8,128)}, f32[1,512,1,512]{3,1,2,0:T(8,128)S(1)}, u32[]{:S(2)}) copy-start(f32[1,512,1,512]{3,1,2,0:T(8,128)S(1)} %copy.38) | copy-start | bytes 3145732
  2.2 2.7 collective-permute-start.1
  3.9 1.0 copy-start.15
  4.9 39.6 %copy-start.16 = (f32[512,512]{1,0:T(8,128)S(1)}, f32[512,512]{1,0:T(8,128)}, u32[]{:S(2)}) copy-start(f32[512,512]{1,0:T(8,128)} %copy-done.15) | copy-start | bytes 3145732
  9.4 61.4 %copy-start.2 = (f32[512,512]{1,0:T(8,128)}, f32[512,512]{1,0:T(8,128)S(1)}, u32[]{:S(2)}) copy-start(f32[512,512]{1,0:T(8,128)S(1)} %get-tuple-element.49.l12_ref) | copy-start | bytes 3145732
  9.4 31.0 %collective-permute-start.2 = (f32[512,512]{1,0:T(8,128)S(1)}, f32[512,512]{1,0:T(8,128)}, u32[]{:S(2)}, u32[]{:S(2)}) collective-permute-start(f32[512,512]{1,0:T(8,128)S(1)} %get-tuple-element.48), channel_id=1, source_target_pairs={{2,0},{3,1},{6,4},{7,5},{10,8},{11,9},{14,12},{15,13},{18,16},{19,... | collective-permute-start | bytes 3145736 | tf_op jit(solution)/shard_map/ppermute | solution.py:219
  10.7 32.0 %collective-permute-start.5 = (f32[512,512]{1,0:T(8,128)S(1)}, f32[512,512]{1,0:T(8,128)}, u32[]{:S(2)}, u32[]{:S(2)}) collective-permute-start(f32[512,512]{1,0:T(8,128)S(1)} %get-tuple-element.46), channel_id=1, source_target_pairs={{2,6},{3,7}} | collective-permute-start | bytes 3145736 | tf_op jit(solution)/shard_map/ppermute | solution.py:219
  40.4 16.5 %collective-permute-start.3 = (f32[512,512]{1,0:T(8,128)}, f32[512,512]{1,0:T(8,128)}, u32[]{:S(2)}, u32[]{:S(2)}) collective-permute-start(f32[512,512]{1,0:T(8,128)} %collective-permute-done.2), channel_id=1, source_target_pairs={{0,1},{1,0},{4,5},{5,4},{8,9},{9,8},{12,13},{13,12},{16,17},{17,16... | collective-permute-start | bytes 3145736 | tf_op jit(solution)/shard_map/ppermute | solution.py:219
  42.7 24.9 %collective-permute-start.6 = (f32[512,512]{1,0:T(8,128)}, f32[512,512]{1,0:T(8,128)}, u32[]{:S(2)}, u32[]{:S(2)}) collective-permute-start(f32[512,512]{1,0:T(8,128)} %collective-permute-done.5), channel_id=1, source_target_pairs={{6,7},{7,6}} | collective-permute-start | bytes 3145736 | tf_op jit(solution)/shard_map/ppermute | solution.py:219
  47.5 1.2 copy-start.17
  48.6 8.3 %copy-start.13 = (f32[512,512]{1,0:T(8,128)S(1)}, f32[512,512]{1,0:T(8,128)}, u32[]{:S(2)}) copy-start(f32[512,512]{1,0:T(8,128)} %get-tuple-element.50.k1_ref) | copy-start | bytes 3145732
  48.6 32.6 %all-to-all-start = ((f32[16,3,32,256]{3,2,1,0:T(8,128)}), f32[16,3,32,256]{3,2,1,0:T(8,128)}, u32[]{:S(2)}, u32[]{:S(2)}) async-start(f32[16,3,32,256]{3,2,1,0:T(8,128)} %copy-done.17), calls=%async_computation | async-start | bytes 3145728 | tf_op jit(solution)/shard_map/all_to_all | solution.py:256
  56.9 4.7 %copy-start.24 = (f32[512,512]{1,0:T(8,128)S(1)}, f32[512,512]{1,0:T(8,128)}, u32[]{:S(2)}) copy-start(f32[512,512]{1,0:T(8,128)} %get-tuple-element.47.y_ref) | copy-start | bytes 3145732
  67.6 3.2 %copy-start.18 = (f32[512,512]{1,0:T(8,128)}, f32[512,512]{1,0:T(8,128)S(1)}, u32[]{:S(2)}) copy-start(f32[512,512]{1,0:T(8,128)S(1)} %get-tuple-element.11.x_ref) | copy-start | bytes 3145732
  70.8 7.7 %copy-start.4 = (f32[512,512]{1,0:T(8,128)}, f32[512,512]{1,0:T(8,128)S(1)}, u32[]{:S(2)}) copy-start(f32[512,512]{1,0:T(8,128)S(1)} %get-tuple-element.29.k2_ref) | copy-start | bytes 3145732
  77.4 1.0 copy-start.23
  78.4 1.4 copy-start.11
  78.5 15.9 %collective-permute-start.7 = (f32[256,512]{1,0:T(8,128)S(1)}, f32[256,512]{1,0:T(8,128)S(1)}, u32[]{:S(2)}, u32[]{:S(2)}) collective-permute-start(f32[256,512]{1,0:T(8,128)S(1)} %slice_select_fusion.3), channel_id=1, source_target_pairs={{6,0},{7,1}} | collective-permute-start | bytes 1572872 | tf_op jit(solution)/shard_map/ppermute | solution.py:219
  79.8 14.6 %collective-permute-start.8 = (f32[256,512]{1,0:T(8,128)S(1)}, f32[256,512]{1,0:T(8,128)}, u32[]{:S(2)}, u32[]{:S(2)}) collective-permute-start(f32[256,512]{1,0:T(8,128)S(1)} %slice_select_fusion.3), channel_id=1, source_target_pairs={{6,2},{7,3}} | collective-permute-start | bytes 1572872 | tf_op jit(solution)/shard_map/ppermute | solution.py:219
  82.7 15.7 %collective-permute-start.4 = (f32[3,32,256]{2,1,0:T(8,128)S(1)}, f32[3,32,256]{2,1,0:T(8,128)S(1)}, u32[]{:S(2)}, u32[]{:S(2)}) collective-permute-start(f32[3,32,256]{2,1,0:T(8,128)S(1)} %reduce_sum.18), channel_id=1, source_target_pairs={{0,16},{16,0},{1,17},{17,1},{2,18},{18,2},{3,19},{19,3},{4,20},{20... | collective-permute-start | bytes 294920 | tf_op jit(solution)/shard_map/ppermute | solution.py:235
  94.5 5.4 %collective-permute-start.9 = (f32[256,512]{1,0:T(8,128)S(1)}, f32[256,512]{1,0:T(8,128)S(1)}, u32[]{:S(2)}, u32[]{:S(2)}) collective-permute-start(f32[256,512]{1,0:T(8,128)S(1)} %broadcast_select_fusion.11), channel_id=1, source_target_pairs={{0,1},{1,0},{2,3},{3,2}} | collective-permute-start | bytes 1572872 | tf_op jit(solution)/shard_map/ppermute | solution.py:219
  98.5 1.6 copy-start.3
  98.5 1.6 copy-start.9
  98.5 1.8 copy-start.19
  100.1 4.0 %copy-start.5 = (f32[512,512]{1,0:T(8,128)}, f32[512,512]{1,0:T(8,128)S(1)}, u32[]{:S(2)}) copy-start(f32[512,512]{1,0:T(8,128)S(1)} %pad_maximum_fusion.x12_ref) | copy-start | bytes 3145732
  157.4 2.7 copy-start.25
  160.1 19.9 %collective-permute-start.11 = (f32[16,2,32,512]{3,2,1,0:T(8,128)}, f32[16,2,32,512]{3,2,1,0:T(8,128)}, u32[]{:S(2)}, u32[]{:S(2)}) collective-permute-start(f32[16,2,32,512]{3,2,1,0:T(8,128)} %slice.77), channel_id=1, source_target_pairs={{6,7},{7,6}} | collective-permute-start | bytes 6291464 | tf_op jit(solution)/shard_map/ppermute | solution.py:219
  164.7 7.2 %collective-permute-start.10 = (f32[4,32,512]{2,1,0:T(8,128)S(1)}, f32[4,32,512]{2,1,0:T(8,128)S(1)}, u32[]{:S(2)}, u32[]{:S(2)}) collective-permute-start(f32[4,32,512]{2,1,0:T(8,128)S(1)} %reduce_sum.19), channel_id=1, source_target_pairs={{0,16},{16,0},{1,17},{17,1},{2,18},{18,2},{3,19},{19,3},{4,20},{20... | collective-permute-start | bytes 786440 | tf_op jit(solution)/shard_map/ppermute | solution.py:235
  174.5 122.4 %all-to-all-start.2 = ((f32[16,4,32,512]{3,2,1,0:T(8,128)}), f32[16,4,32,512]{3,2,1,0:T(8,128)}, u32[]{:S(2)}, u32[]{:S(2)}) async-start(f32[16,4,32,512]{3,2,1,0:T(8,128)} %broadcast_in_dim.12), calls=%async_computation.2 | async-start | bytes 8388608 | tf_op jit(solution)/shard_map/all_to_all | solution.py:320
  197.5 3.4 %copy-start.29 = (f32[16,1,32,1,256]{4,3,2,1,0:T(1,128)S(1)}, f32[16,1,32,1,256]{4,3,2,1,0:T(1,128)}, u32[]{:S(2)}) copy-start(f32[16,1,32,1,256]{4,3,2,1,0:T(1,128)} %get-tuple-element.32) | copy-start | bytes 1572868
  200.8 1.0 copy-start.28
  201.9 1.2 copy-start.14
  201.9 1.5 copy-start.20
  203.4 2.1 copy-start.27
  205.5 1.2 copy-start.22
  209.9 1.0 copy-start
  210.9 1.2 copy-start.12
  210.9 1.5 copy-start.21
  218.5 5.8 %copy-start.1 = (f32[512,512]{1,0:T(8,128)S(1)}, f32[512,512]{1,0:T(8,128)}, u32[]{:S(2)}) copy-start(f32[512,512]{1,0:T(8,128)} %copy-done) | copy-start | bytes 3145732
  223.4 46.7 %copy-start.10 = (f32[1,512,1,512]{3,1,2,0:T(8,128)S(1)}, f32[1,512,1,512]{3,1,2,0:T(8,128)}, u32[]{:S(2)}) copy-start(f32[1,512,1,512]{3,1,2,0:T(8,128)} %copy-done.8) | copy-start | bytes 3145732
  223.4 50.9 %collective-permute-start.21 = (f32[512,512]{1,0:T(8,128)S(1)}, f32[512,512]{1,0:T(8,128)S(1)}, u32[]{:S(2)}, u32[]{:S(2)}) collective-permute-start(f32[512,512]{1,0:T(8,128)S(1)} %get-tuple-element.16), channel_id=1, source_target_pairs={{6,2}} | collective-permute-start | bytes 3145736 | tf_op jit(solution)/shard_map/ppermute | solution.py:219
  224.4 45.8 %collective-permute-start.18 = (f32[256,512]{1,0:T(8,128)S(1)}, f32[256,512]{1,0:T(8,128)S(1)}, u32[]{:S(2)}, u32[]{:S(2)}) collective-permute-start(f32[256,512]{1,0:T(8,128)S(1)} %slice_select_fusion), channel_id=1, source_target_pairs={{6,0},{7,1}} | collective-permute-start | bytes 1572872 | tf_op jit(solution)/shard_map/ppermute | solution.py:219
  225.7 45.8 %collective-permute-start.16 = (f32[256,512]{1,0:T(8,128)S(1)}, f32[256,512]{1,0:T(8,128)S(1)}, u32[]{:S(2)}, u32[]{:S(2)}) collective-permute-start(f32[256,512]{1,0:T(8,128)S(1)} %slice_select_fusion), channel_id=1, source_target_pairs={{6,4},{7,5}} | collective-permute-start | bytes 1572872 | tf_op jit(solution)/shard_map/ppermute | solution.py:219
  226.5 37.7 %collective-permute-start.14 = (f32[256,512]{1,0:T(8,128)S(1)}, f32[256,512]{1,0:T(8,128)S(1)}, u32[]{:S(2)}, u32[]{:S(2)}) collective-permute-start(f32[256,512]{1,0:T(8,128)S(1)} %slice_select_fusion.1), channel_id=1, source_target_pairs={{6,0},{7,1}} | collective-permute-start | bytes 1572872 | tf_op jit(solution)/shard_map/ppermute | solution.py:219
  227.8 45.8 %collective-permute-start.12 = (f32[256,512]{1,0:T(8,128)S(1)}, f32[256,512]{1,0:T(8,128)S(1)}, u32[]{:S(2)}, u32[]{:S(2)}) collective-permute-start(f32[256,512]{1,0:T(8,128)S(1)} %slice_select_fusion.2), channel_id=1, source_target_pairs={{6,4},{7,5}} | collective-permute-start | bytes 1572872 | tf_op jit(solution)/shard_map/ppermute | solution.py:219
  264.1 12.1 %collective-permute-start.15 = (f32[256,512]{1,0:T(8,128)S(1)}, f32[256,512]{1,0:T(8,128)S(1)}, u32[]{:S(2)}, u32[]{:S(2)}) collective-permute-start(f32[256,512]{1,0:T(8,128)S(1)} %collective-permute-done.14), channel_id=1, source_target_pairs={{0,1},{1,0}} | collective-permute-start | bytes 1572872 | tf_op jit(solution)/shard_map/ppermute | solution.py:219
  270.1 26.8 %collective-permute-start.20 = (f32[512,512]{1,0:T(8,128)S(1)}, f32[512,512]{1,0:T(8,128)}, u32[]{:S(2)}, u32[]{:S(2)}) collective-permute-start(f32[512,512]{1,0:T(8,128)S(1)} %bitcast.54), channel_id=1, source_target_pairs={{4,0},{5,1}} | collective-permute-start | bytes 3145736 | tf_op jit(solution)/shard_map/ppermute | solution.py:219
  271.5 6.2 %collective-permute-start.19 = (f32[256,512]{1,0:T(8,128)S(1)}, f32[256,512]{1,0:T(8,128)S(1)}, u32[]{:S(2)}, u32[]{:S(2)}) collective-permute-start(f32[256,512]{1,0:T(8,128)S(1)} %collective-permute-done.18), channel_id=1, source_target_pairs={{0,1},{1,0}} | collective-permute-start | bytes 1572872 | tf_op jit(solution)/shard_map/ppermute | solution.py:219
  273.6 4.2 %collective-permute-start.17 = (f32[256,512]{1,0:T(8,128)S(1)}, f32[256,512]{1,0:T(8,128)S(1)}, u32[]{:S(2)}, u32[]{:S(2)}) collective-permute-start(f32[256,512]{1,0:T(8,128)S(1)} %collective-permute-done.16), channel_id=1, source_target_pairs={{4,5},{5,4}} | collective-permute-start | bytes 1572872 | tf_op jit(solution)/shard_map/ppermute | solution.py:219
  274.3 2.0 collective-permute-start.13
  296.9 1.2 copy-start.7

commit v2 on v1

v2 whole, which is shorter than its diff:
```python
import jax
import jax.numpy as jnp
from jax import lax
from jax.sharding import Mesh
from jax.sharding import PartitionSpec as P
from jax.experimental import pallas as pl
from jax.experimental.pallas import tpu as pltpu

N = 512
H = 256
ALL = ("y", "xh", "z", "xl", "core")
PLANE = ("y", "z")
F32 = jnp.float32
BF16 = jnp.bfloat16


def dev(row, column):
    return row * 4 + column


def split(x):
    hi = x.astype(BF16)
    return hi, (x - hi.astype(F32)).astype(BF16)


def as_parts(x):
    return x if isinstance(x, tuple) else split(x)


def mm(a, b, ta=False):
    ah, al = as_parts(a)
    bh, bl = as_parts(b)
    dims = (((0 if ta else 1,), (0,)), ((), ()))

    def dot(u, v):
        return lax.dot_general(u, v, dims, preferred_element_type=F32)

    return dot(ah, bh) + (dot(ah, bl) + dot(al, bh))


def iotas(n):
    return (
        lax.broadcasted_iota(jnp.int32, (n, n), 0),
        lax.broadcasted_iota(jnp.int32, (n, n), 1),
    )


def tril(x):
    i, j = iotas(x.shape[0])
    return jnp.where(i >= j, x, 0.0)


def sym_half(p):
    i, j = iotas(p.shape[0])
    low = jnp.where(i > j, p, jnp.where(i == j, 0.5 * p, 0.0))
    return 0.5 * (low + low.T)


def inverse_lower(k_ref, out_ref):
    b = 128
    i, j = iotas(b)
    inv, blocks = [], []
    for s in range(4):
        t = k_ref[s * b:(s + 1) * b, s * b:(s + 1) * b]
        on = jnp.where(i == j, t, 0.0)
        down = 1.0 / jnp.sum(on, axis=1, keepdims=True)
        across = 1.0 / jnp.sum(on, axis=0, keepdims=True)
        off = (i // 2 == j // 2) & (i > j)
        inv.append(jnp.where(i == j, down, 0.0) - jnp.where(off, down * t * across, 0.0))
        blocks.append(t)
    size = 2
    while size < b:
        off = (i // (2 * size) == j // (2 * size)) & (i // size > j // size)
        parts = [split(x) for x in inv]
        half = [mm(jnp.where(off, t, 0.0), x) for t, x in zip(blocks, parts)]
        inv = [x - mm(p, h) for x, p, h in zip(inv, parts, half)]
        size *= 2
    out_ref[...] = jnp.zeros((N, N), F32)
    for s in range(4):
        out_ref[s * b:(s + 1) * b, s * b:(s + 1) * b] = inv[s]
    for s in (0, 2):
        low = k_ref[(s + 1) * b:(s + 2) * b, s * b:(s + 1) * b]
        out_ref[(s + 1) * b:(s + 2) * b, s * b:(s + 1) * b] = -mm(inv[s + 1], mm(low, inv[s]))
    top = out_ref[:H, :H]
    bottom = out_ref[H:, H:]
    out_ref[H:, :H] = -mm(bottom, mm(k_ref[H:, :H], top))


class Bank:
    def __init__(self, buf, sem):
        self.buf, self.sem = buf, sem

    def at(self, slot):
        return self.buf.at[slot]

    def start(self, slot, src):
        pltpu.make_async_copy(flat(src), self.buf.at[slot], self.sem.at[slot]).start()

    def start_half(self, slot, src, lo):
        pltpu.make_async_copy(
            flat(src).at[:, lo:lo + H], self.buf.at[slot, :, :H], self.sem.at[slot]).start()

    def wait(self, *slots):
        for s in slots:
            pltpu.make_async_copy(self.buf.at[s], self.buf.at[s], self.sem.at[s]).wait()

    def wait_half(self, *slots):
        for s in slots:
            half = self.buf.at[s, :, :H]
            pltpu.make_async_copy(half, half, self.sem.at[s]).wait()

    def get(self, slot):
        return self.buf[slot]


def flat(ref):
    return ref.at[0, :, 0, :] if len(ref.shape) == 4 else ref


def odd_top(row, xl, core):
    return (xl == 1) & (row <= 1)


def odd_zero(row, xl, core):
    return (xl == 1) & (row == 0)


def odd_one(row, xl, core):
    return (xl == 1) & (row == 1)


LIMIT = 58 * 1024 * 1024


def call(kernel, outs, *args, slots=1, near=(), only=None):
    vm = pl.BlockSpec(memory_space=pltpu.VMEM)
    sm = pl.BlockSpec(memory_space=pltpu.SMEM)
    far = pl.BlockSpec(memory_space=pl.ANY)
    n, m = len(args), len(outs)

    def body(*refs):
        ins, out_refs, built = refs[:n], refs[n:n + m], refs[n + m:n + 2 * m]
        buf, sem, done = refs[n + 2 * m:]
        kernel(*ins, *built, buf, sem)
        copies = [pltpu.make_async_copy(b, flat(o), done.at[i]) for i, (b, o) in enumerate(zip(built, out_refs))]

        def store():
            for c in copies:
                c.start()
            for c in copies:
                c.wait()

        if only is None:
            store()
        else:
            pl.when(only(*(ins[0][i] for i in range(3))))(store)

    return pl.pallas_call(
        body,
        out_shape=[jax.ShapeDtypeStruct(s, F32) for s in outs],
        in_specs=[sm if a.dtype == jnp.int32 else vm if i in near else far for i, a in enumerate(args)],
        out_specs=[far] * m,
        scratch_shapes=[pltpu.VMEM((s[1], s[3]) if len(s) == 4 else s, F32) for s in outs] + [
            pltpu.VMEM((slots, N, N), F32), pltpu.SemaphoreType.DMA((slots,)), pltpu.SemaphoreType.DMA((m,))],
        compiler_params=pltpu.CompilerParams(vmem_limit_bytes=LIMIT),
    )(*args)


def k_sum_odd(pos_ref, a_ref, asw_ref, l_ref, lsw_ref, out_ref, buf, sem):
    row, xl, core = pos_ref[0], pos_ref[1], pos_ref[2]
    bank = Bank(buf, sem)
    live = (row >= 1) & (xl == 1)

    def begin(a3, a2, l3, l2, lo):
        bank.start(0, a3)
        bank.start_half(1, l3, lo)
        bank.start_half(2, l2, lo)
        bank.start(3, a2)

    @pl.when(live & (core == 0))
    def _():
        begin(asw_ref, a_ref, lsw_ref, l_ref, 0)

    @pl.when(live & (core == 1))
    def _():
        begin(a_ref, asw_ref, l_ref, lsw_ref, H)

    @pl.when(live)
    def _():
        bank.wait(0)
        a3 = split(jnp.where(row == 1, 0.0, bank.get(0)))
        bank.wait_half(1)
        out_ref[:, :, :H] = mm(a3, buf[1, :, :H], ta=True).reshape(16, 32, H)
        bank.wait_half(2)
        l2 = split(buf[2, :, :H])
        out_ref[:, :, H:N] = mm(a3, l2, ta=True).reshape(16, 32, H)
        bank.wait(3)
        out_ref[:, :, N:] = mm(bank.get(3), l2, ta=True).reshape(16, 32, H)

    @pl.when(jnp.logical_not(live))
    def _():
        out_ref[...] = jnp.zeros(out_ref.shape, F32)


def k_first(pos_ref, l_ref, lsw_ref, inv_ref, x12_ref, buf, sem):
    row, xl, core = pos_ref[0], pos_ref[1], pos_ref[2]
    bank = Bank(buf, sem)
    live = (xl == 1) & (row <= 1)

    @pl.when(live & (row == core))
    def _():
        bank.start(0, l_ref)
        bank.start(1, lsw_ref)

    @pl.when(live & (row != core))
    def _():
        bank.start(0, lsw_ref)
        bank.start(1, l_ref)

    @pl.when(live)
    def _():
        bank.wait(0)
        inverse_lower(bank.at(0), inv_ref)
        bank.wait(1)
        x12_ref[...] = mm(inv_ref[...], bank.get(1))


def k_second(pos_ref, l_ref, kq_ref, kqsw_ref, first_ref, x12_ref, inv_ref, x_ref, out_ref, buf, sem):
    row, xl, core = pos_ref[0], pos_ref[1], pos_ref[2]
    bank = Bank(buf, sem)
    even = (xl == 0) & (row <= 1)
    odd = (xl == 1) & (row <= 1)

    @pl.when(even & (row == core))
    def _():
        bank.start(0, kq_ref)

    @pl.when(even & (row != core))
    def _():
        bank.start(0, kqsw_ref)

    @pl.when(even)
    def _():
        bank.start(1, l_ref)

    @pl.when(even & (core == 0))
    def _():
        bank.start_half(2, kq_ref, 0)

    @pl.when(even & (core == 1))
    def _():
        bank.start_half(2, kqsw_ref, H)

    @pl.when(odd & (row == 1) & (core == 0))
    def _():
        bank.start(1, x12_ref)

    @pl.when(odd & (row == core))
    def _():
        bank.start(1, first_ref)

    @pl.when(even)
    def _():
        bank.wait(0)
        inverse_lower(bank.at(0), inv_ref)
        bank.wait(1)
        inv = split(inv_ref[...])
        x = mm(inv, bank.get(1))
        x_ref[...] = x
        out_ref[:, :, :N] = x.reshape(16, 32, N)
        bank.wait_half(2)
        half = jnp.where(row == 1, mm(inv, buf[2, :, :H]), 0.0)
        out_ref[:, :, N:] = half.reshape(16, 32, H)

    @pl.when(odd & ((row == 1) | (core == 0)))
    def _():
        bank.wait(1)
        out_ref[:, :, :N] = bank.get(1).reshape(16, 32, N)
        out_ref[:, :, N:] = jnp.zeros((16, 32, H), F32)

    @pl.when((row >= 2) | ((xl == 1) & (row == 0) & (core == 1)))
    def _():
        out_ref[...] = jnp.zeros(out_ref.shape, F32)


def k_send(pos_ref, ac_ref, acsw_ref, l_ref, part_ref, other_ref, out_ref, buf, sem):
    row, xl, core = pos_ref[0], pos_ref[1], pos_ref[2]
    bank = Bank(buf, sem)
    live = (xl == 0) & (row >= 1)

    @pl.when(live & (core == 0))
    def _():
        bank.start(0, acsw_ref)
        bank.start(2, ac_ref)

    @pl.when(live & (core == 1))
    def _():
        bank.start(0, ac_ref)
        bank.start(2, acsw_ref)

    @pl.when(live)
    def _():
        bank.start(1, l_ref)
        bank.wait(0, 1)
        l = split(bank.get(1))
        a3 = jnp.where(row == 1, 0.0, bank.get(0))
        out_ref[:, :, :N] = mm(a3, l, ta=True).reshape(16, 32, N)
        bank.wait(2)
        out_ref[:, :, N:] = mm(bank.get(2), l, ta=True).reshape(16, 32, N)

    @pl.when(xl == 1)
    def _():
        s = part_ref[...] + other_ref[...]
        out_ref[:, :, :N + H] = jnp.broadcast_to(s[None], (16, 32, N + H))
        out_ref[:, :, N + H:] = jnp.zeros((16, 32, H), F32)

    @pl.when((xl == 0) & (row == 0))
    def _():
        out_ref[...] = jnp.zeros(out_ref.shape, F32)


def k_own(got_ref, out_ref, buf, sem):
    total = got_ref[0]
    for s in range(1, 16):
        total = total + got_ref[s]
    out_ref[...] = total


def k_spread(a_ref, b_ref, out_ref, buf, sem):
    s = a_ref[...] + b_ref[...]
    out_ref[...] = jnp.broadcast_to(s[None], out_ref.shape)


def gather_tile(bank, slot, core, got_ref, gotsw_ref, lo):
    def begin(left, right):
        for half, src in ((0, left), (H, right)):
            for s in range(16):
                pltpu.make_async_copy(
                    src.at[s, :, lo:lo + H],
                    bank.buf.at[slot, s * 32:(s + 1) * 32, half:half + H],
                    bank.sem.at[slot]).start()

    @pl.when(core == 0)
    def _():
        begin(got_ref, gotsw_ref)

    @pl.when(core == 1)
    def _():
        begin(gotsw_ref, got_ref)


def k_chain_a(pos_ref, got_ref, gotsw_ref, a_ref, asw_ref, l_ref, lsw_ref, i1_ref, x12_ref, sym_ref, ap_ref, out_ref, half_ref, buf, sem):
    row, xl, core = pos_ref[0], pos_ref[1], pos_ref[2]
    bank = Bank(buf, sem)
    live = (xl == 1) & (row == 1)

    @pl.when(live)
    def _():
        gather_tile(bank, 0, core, got_ref, gotsw_ref, 0)
        bank.start(1, i1_ref)

        @pl.when(core == 0)
        def _():
            bank.start(2, asw_ref)
            bank.start(3, lsw_ref)
            bank.start(6, a_ref)

        @pl.when(core == 1)
        def _():
            bank.start(2, a_ref)
            bank.start(3, l_ref)
            bank.start(6, asw_ref)

        gather_tile(bank, 4, core, got_ref, gotsw_ref, H)
        bank.start(5, x12_ref)
        bank.wait(0, 1, 2, 3)
        i1 = split(bank.get(1))
        g = tril(bank.get(2) - mm(i1, bank.get(0), ta=True))
        sym = sym_half(mm(tril(bank.get(3)), g, ta=True))
        sym_ref[...] = sym
        bank.wait(4, 5, 6)
        inner = bank.get(4) + 2.0 * mm(sym, bank.get(5))
        ap_ref[...] = bank.get(6) - mm(i1, inner, ta=True)
        lo = pl.multiple_of(core * H, H)
        buf[4] = inner
        half_ref[...] = sym_ref[pl.ds(lo, H), :]
        out_ref[:H, :] = half_ref[...]
        out_ref[H:, :] = buf[4, pl.ds(lo, H), :]


def k_chain_b(pos_ref, got_ref, gotsw_ref, a_ref, asw_ref, l_ref, lsw_ref, i2_ref, x12_ref, x12sw_ref, half_ref, halfsw_ref, sym_ref, out_ref, buf, sem):
    row, xl, core = pos_ref[0], pos_ref[1], pos_ref[2]
    bank = Bank(buf, sem)
    live = (xl == 1) & (row == 0)

    def stack(up, down):
        pltpu.make_async_copy(up, buf.at[0, :H], sem.at[0]).start()
        pltpu.make_async_copy(down, buf.at[0, H:], sem.at[0]).start()

    @pl.when(live)
    def _():
        @pl.when(core == 0)
        def _():
            stack(half_ref, halfsw_ref)
            bank.start(1, x12_ref)

        @pl.when(core == 1)
        def _():
            stack(halfsw_ref, half_ref)
            bank.start(1, x12sw_ref)

        gather_tile(bank, 2, core, got_ref, gotsw_ref, H)
        gather_tile(bank, 3, core, got_ref, gotsw_ref, N)
        bank.start(4, i2_ref)

        @pl.when(core == 0)
        def _():
            bank.start(5, a_ref)
            bank.start(6, l_ref)

        @pl.when(core == 1)
        def _():
            bank.start(5, asw_ref)
            bank.start(6, lsw_ref)

        bank.wait(0, 1, 2)
        x12 = split(bank.get(1))
        buf[7] = bank.get(2) + 2.0 * mm(bank.get(0), x12)
        inner = mm(x12, bank.get(7), ta=True) + mm(bank.get(2), x12, ta=True)
        bank.wait(3, 4, 5, 6)
        g = tril(bank.get(5) - mm(bank.get(4), bank.get(3) - inner, ta=True))
        sym_ref[...] = sym_half(mm(tril(bank.get(6)), g, ta=True))
        lo = pl.multiple_of(core * H, H)
        out_ref[:H, :] = sym_ref[pl.ds(lo, H), :]
        out_ref[H:, :] = buf[7, pl.ds(lo, H), :]


def k_chain_c(pos_ref, sym1_ref, sym2_ref, inv_ref, e_ref, buf, sem):
    row, xl, core = pos_ref[0], pos_ref[1], pos_ref[2]
    bank = Bank(buf, sem)

    @pl.when((xl == 1) & (row == 0) & (core == 0))
    def _():
        bank.start(0, sym2_ref)

    @pl.when((xl == 1) & (row == 1) & (core == 1))
    def _():
        bank.start(0, sym1_ref)

    @pl.when((xl == 1) & (((row == 1) & (core == 1)) | ((row == 0) & (core == 0))))
    def _():
        bank.start(1, inv_ref)
        bank.wait(0, 1)
        inv = split(bank.get(1))
        e_ref[...] = mm(inv, mm(bank.get(0), inv), ta=True)


def k_final(pos_ref, a_ref, asw_ref, ac_ref, acsw_ref, xs_ref, xh_ref, inv_ref, x_ref, one_ref, onesw_ref, zero_ref, zerosw_ref, ap_ref, e_ref, *rest):
    ts_ref, res, buf, sem = rest
    row, xl, core = pos_ref[0], pos_ref[1], pos_ref[2]
    bank = Bank(buf, sem)
    X1, X2, X12, A, A3, A2 = 0, 1, 2, 3, 4, 5
    SYM, W, T, INV, XOWN, L1 = 2, 4, 5, 6, 7, 8

    def rows_of(slot, src, lo, width):
        for s in range(16):
            pltpu.make_async_copy(
                src.at[s, :, lo:lo + width], bank.buf.at[slot, s * 32:(s + 1) * 32, :width],
                bank.sem.at[slot]).start()

    def sums(slot, lo):
        rows_of(slot, ts_ref, lo, N)

    def x2(slot):
        bank.start(slot, xs_ref.at[:, :N])

    def x1(slot):
        bank.start(slot, xs_ref.at[:, N:2 * N])

    def x12(slot):
        for c, (left, right) in enumerate(((0, H), (H, 0))):
            @pl.when(core == c)
            def _():
                pltpu.make_async_copy(
                    xs_ref.at[:, 2 * N:], bank.buf.at[slot, :, left:left + H], bank.sem.at[slot]).start()
                pltpu.make_async_copy(
                    xh_ref, bank.buf.at[slot, :, right:right + H], bank.sem.at[slot]).start()

    def stack(slot, lo, here, there):
        for c, (up, down) in enumerate(((here, there), (there, here))):
            @pl.when(core == c)
            def _():
                pltpu.make_async_copy(
                    up.at[lo:lo + H], bank.buf.at[slot, :H], bank.sem.at[slot]).start()
                pltpu.make_async_copy(
                    down.at[lo:lo + H], bank.buf.at[slot, H:], bank.sem.at[slot]).start()

    low_even = (row >= 2) & (xl == 0)

    @pl.when(low_even)
    def _():
        @pl.when(core == 0)
        def _():
            bank.start(A3, acsw_ref)
            bank.start(A2, ac_ref)

        @pl.when(core == 1)
        def _():
            bank.start(A3, ac_ref)
            bank.start(A2, acsw_ref)

        x12(X12)
        x1(X1)
        x2(X2)
        bank.start(A, a_ref)
        bank.wait(A3, A2, X12)
        a3 = split(bank.get(A3))
        moved = bank.get(A2) - mm(a3, bank.get(X12))
        bank.wait(X1, A)
        res[...] = bank.get(A) - mm(a3, bank.get(X1))
        bank.wait(X2)
        res[...] -= mm(moved, bank.get(X2))

    @pl.when((row >= 2) & (xl == 1) & (core == 0))
    def _():
        bank.start(A3, asw_ref)
        x1(X1)
        bank.start(A, a_ref)
        x2(X2)
        bank.wait(A3, X1, A)
        moved = bank.get(A) - mm(bank.get(A3), bank.get(X1))
        bank.wait(X2)
        res[...] = mm(moved, bank.get(X2))

    @pl.when((row >= 2) & (xl == 1) & (core == 1))
    def _():
        bank.start(A, a_ref)
        x1(X1)
        bank.wait(A, X1)
        res[...] = mm(bank.get(A), bank.get(X1))

    @pl.when((row == 1) & (xl == 0))
    def _():
        bank.start(INV, inv_ref)

        @pl.when(core == 0)
        def _():
            bank.start(L1, ac_ref)

        @pl.when(core == 1)
        def _():
            bank.start(L1, acsw_ref)

        stack(W, H, one_ref, onesw_ref)
        x2(X2)
        stack(SYM, 0, one_ref, onesw_ref)
        bank.start(XOWN, x_ref)
        sums(T, 0)
        bank.start(A, a_ref)
        bank.wait(INV, L1, W)
        inv = split(bank.get(INV))
        ap = bank.get(L1) - mm(inv, bank.get(W), ta=True)
        bank.wait(X2)
        side = mm(ap, bank.get(X2))
        bank.wait(SYM, XOWN)
        inner = 2.0 * mm(bank.get(SYM), bank.get(XOWN))
        bank.wait(T, A)
        res[...] = bank.get(A) - side - mm(inv, inner + bank.get(T), ta=True)

    @pl.when((row == 0) & (xl == 0))
    def _():
        sums(T, 0)
        x12(L1)
        stack(W, H, zero_ref, zerosw_ref)
        x1(X1)
        stack(SYM, 0, zero_ref, zerosw_ref)
        bank.start(XOWN, x_ref)
        sums(X2, N)
        bank.start(INV, inv_ref)
        bank.start(A, a_ref)
        bank.wait(T, L1)
        inner = -mm(bank.get(L1), bank.get(T), ta=True)
        bank.wait(W, X1)
        inner = inner - mm(bank.get(W), bank.get(X1), ta=True)
        bank.wait(SYM, XOWN)
        inner = inner + 2.0 * mm(bank.get(SYM), bank.get(XOWN))
        bank.wait(X2, INV, A)
        res[...] = bank.get(A) - mm(bank.get(INV), inner + bank.get(X2), ta=True)

    @pl.when((row == 1) & (xl == 1) & (core == 0))
    def _():
        bank.start(A, ap_ref)
        x2(X2)
        bank.wait(A, X2)
        res[...] = mm(bank.get(A), bank.get(X2))

    def keep(src):
        bank.start(A, src)
        bank.wait(A)
        res[...] = bank.get(A)

    @pl.when((row == 1) & (xl == 1) & (core == 1))
    def _():
        keep(e_ref)

    @pl.when((row == 0) & (xl == 1) & (core == 0))
    def _():
        keep(e_ref)

    @pl.when((row == 0) & (xl == 1) & (core == 1))
    def _():
        keep(a_ref)


def move(x, pairs):
    return lax.ppermute(x, ALL, [(dev(*a), dev(*b)) for a, b in pairs])


def exchange_cores(x, rows, columns):
    return move(x, [((r, c), (r, c ^ 1)) for r in rows for c in columns])


def swap_xh(x):
    return lax.ppermute(x, "xh", [(0, 1), (1, 0)])


def every(x):
    return lax.all_to_all(x, PLANE, 0, 0, tiled=True)


def local(low, adj):
    rows = range(32)
    below = range(2, 32)
    y, xh, z = (lax.axis_index(n) for n in ("y", "xh", "z"))
    xl, core = lax.axis_index("xl"), lax.axis_index("core")
    pos = jnp.stack([y * 8 + xh * 4 + z, xl, core, z]).astype(jnp.int32)
    tile = (N, N)

    adj_sw = exchange_cores(adj, rows, (2, 3))
    low_sw = exchange_cores(low, rows, (2, 3))
    kq = move(low, [((1, 3), (1, 1)), ((0, 2), (0, 0)), ((1, 2), (1, 0))])
    ac = move(adj, [((r, c), (r, c - 2)) for r in below for c in (2, 3)] + [((1, 2), (1, 0))])

    sums_odd, = call(k_sum_odd, [(16, 32, N + H)], pos, adj, adj_sw, low, low_sw, slots=4)
    got = every(sums_odd)

    inv_odd, x12 = call(k_first, [tile, tile], pos, low, low_sw, slots=2, only=odd_top)
    kq_sw = exchange_cores(kq, (0, 1), (0, 1))
    inv, x, send_x = call(
        k_second, [tile, tile, (16, 32, N + H)], pos, low, kq, kq_sw, inv_odd, x12, slots=3)
    x12_zero = move(x12, [((1, 2), (0, 2))])
    x12_zero_sw = exchange_cores(x12_zero, (0,), (2,))
    got, send_x = lax.optimization_barrier((got, send_x))
    got_x = every(send_x)

    part = jnp.sum(got, axis=0)
    other = swap_xh(part)
    ac_sw = exchange_cores(ac, range(1, 32), (0, 1))
    send, = call(k_send, [(16, 32, 2 * N)], pos, ac, ac_sw, low, part, other, slots=3, near=(4, 5))
    send, got_x = lax.optimization_barrier((send, got_x))
    sums = every(send)
    xs = jnp.concatenate([got_x[0, :, :N], got_x[1]], 1)
    xs = xs + lax.ppermute(xs, "xh", [(0, 1)])
    sums, xs, x12_zero_sw = lax.optimization_barrier((sums, xs, x12_zero_sw))
    xs = lax.all_gather(xs, PLANE, tiled=True)
    sums_sw = exchange_cores(sums[:, :, :N + H], (0, 1), (2, 3))
    sym1, ap, to_one, half = call(
        k_chain_a, [tile, tile, tile, (H, N)], pos, sums, sums_sw, adj, adj_sw, low, low_sw, inv_odd, x12,
        slots=7, only=odd_one)
    sums, to_one, half = lax.optimization_barrier((sums, to_one, half))
    half = move(half, [((1, c), (0, c)) for c in (2, 3)])
    one = move(to_one, [((1, 2), (1, 0)), ((1, 3), (1, 1))])
    half_sw = exchange_cores(half, (0,), (2, 3))
    sym2, to_zero = call(
        k_chain_b, [tile, tile], pos, sums, sums_sw, adj, adj_sw, low, low_sw, inv_odd, x12_zero, x12_zero_sw,
        half, half_sw, slots=8, only=odd_zero)
    zero = move(to_zero, [((0, 2), (0, 0)), ((0, 3), (0, 1))])

    own, = call(k_own, [(32, 2 * N)], sums, near=(0,))
    send, = call(
        k_spread, [(16, 32, 2 * N)], own, lax.ppermute(own, "xh", [(1, 0)]), near=(0, 1))
    ts = every(send)

    e, = call(k_chain_c, [tile], pos, sym1, sym2, inv_odd, slots=2, only=odd_top)
    one_sw = exchange_cores(one, (1,), (0, 1))
    zero_sw = exchange_cores(zero, (0,), (0, 1))
    xs_sw = exchange_cores(xs[:, 2 * N:], rows, (0, 1))
    out, = call(
        k_final, [adj.shape], pos, adj, adj_sw, ac, ac_sw, xs, xs_sw, inv, x,
        one, one_sw, zero, zero_sw, ap, e, ts, slots=9)
    return out


def solution(mesh):
    fine = Mesh(mesh.devices.reshape(4, 2, 4, 2, 2), ALL)
    placed = P(None, ("y", "xh", "z"), None, ("xl", "core"))
    return jax.shard_map(
        local, mesh=fine, in_specs=(placed, placed), out_specs=placed, check_vma=False
    )
```

time: 312 us -> 214 us (0.69)
  blocking collectives: 53.3 us -> 0 us
  other arithmetic: 27 us -> 1.4 us
  local copies, waits for them, and re-layouts: 34.8 us -> 11.2 us
  starting transfers between devices: 49.4 us -> 65.3 us
  Pallas kernels: 43.2 us -> 29.8 us
  between operations: 0.96 us -> 13.8 us
  waiting for transfers between devices: 99.4 us -> 89 us
    all_to_all x1 -> x0, blocking collectives: 53.3 us -> none  [local(): got = lax.all_to_all(send, PLANE, 0, 0, tiled=True)]
    ppermute x20 -> x18, waiting for transfers between devices: 92.2 us -> 57.7 us  [the longest x16 53 us: move(): return lax.ppermute(x, ALL, [(dev(*a), dev(*b)) for a, b in pairs])]
    all_to_all x2 -> x4, waiting for transfers between devices: 0.01 us -> 28 us  [every(): return lax.all_to_all(x, PLANE, 0, 0, tiled=True)]
    select_n x17 -> x0, other arithmetic: 22.2 us -> none  [the longest x1 5.12 us: local(): left = jnp.where(first, here, there).reshape(16, 2, 32, 2, H)]
    all_to_all x2 -> x4, starting transfers between devices: 13.8 us -> 33 us  [every(): return lax.all_to_all(x, PLANE, 0, 0, tiled=True)]
    pallas_call x9 -> x10, Pallas kernels: 43.2 us -> 29.8 us  [call(): pl.pallas_call(body, out_shape=[jax.ShapeDtypeStruct(s, F32) for s in out...]
    reshape x3 -> x0, local copies, waits for them, and re-layouts: 9.23 us -> none  [the longest x1 3.66 us: local(): rite = jnp.where(first, there, here).reshape(16, 2, 32, 2, H)]
    slice x3 -> x2, local copies, waits for them, and re-layouts: 9.36 us -> 2.01 us  [the longest x1 1.88 us: local(): xs_sw = exchange_cores(xs[:, 2 * N:], rows, (0, 1))]
  transfers between devices with their start and end apart: 24 -> 24, of which waited for: 6 -> 8; matrix products, arithmetic and copies ran while one was open for 13% -> 2% of each run, Pallas kernels for 10% -> 11%
where the time goes in v2:
time: 214 us; the launch traced here: 211 us
  waiting for transfers between devices  89 us (42%)
  starting transfers between devices  65.3 us (31%)
  Pallas kernels  29.8 us (14%)
  between operations  13.8 us (6%)
  local copies, waits for them, and re-layouts  11.2 us (5%)
    ppermute x16, waiting for transfers between devices, move(): return lax.ppermute(x, ALL, [(dev(*a), dev(*b)) for a, b in pairs])  53 us
    all_to_all x4, starting transfers between devices, every(): return lax.all_to_all(x, PLANE, 0, 0, tiled=True)  33 us
    pallas_call x10, Pallas kernels, call(): pl.pallas_call(body, out_shape=[jax.ShapeDtypeStruct(s, F32) for s in out...  29.8 us
    all_to_all x4, waiting for transfers between devices, every(): return lax.all_to_all(x, PLANE, 0, 0, tiled=True)  28 us
    ppermute x16, starting transfers between devices, move(): return lax.ppermute(x, ALL, [(dev(*a), dev(*b)) for a, b in pairs])  25.2 us
    unnamed x30, local copies, waits for them, and re-layouts  7.48 us
    ppermute x1, starting transfers between devices, swap_xh(): return lax.ppermute(x, 'xh', [(0, 1), (1, 0)])  4.43 us
  transfers between devices with their start and end apart: 24, of which 8 were waited for; matrix products, arithmetic and copies ran while one was open for 2% of the time, Pallas kernels for 11%

profile of v2, /device:TPU:1, one launch (start us, length us, event | category | flops | bytes accessed | tf_op | source)
XLA Modules:
  0.0 210.6 jit_solution(7250459590776809948)
XLA Ops:
  6.5 0.7 collective-permute-start.3
  7.3 0.7 collective-permute-start
  8.0 1.6 collective-permute-start.4
  9.6 0.6 pad_add_fusion.refs_0_
  10.2 0.0 collective-permute-done.3.refs_4_.refs_2_.refs_6_
  10.3 0.9 copy-done.1
  11.2 1.0 copy-done.3
  12.2 2.0 shard_map.28
  14.2 0.0 copy-start.2
  14.2 8.7 %all-to-all-start = ((f32[16,32,768]{2,1,0:T(8,128)}), f32[16,32,768]{2,1,0:T(8,128)S(1)}, u32[]{:S(2)}, u32[]{:S(2)}) async-start(f32[16,32,768]{2,1,0:T(8,128)} %shard_map.28), calls=%async_computation | async-start | bytes 3145728 | tf_op jit(solution)/shard_map/all_to_all | solution.py:628
  23.0 7.1 %collective-permute-start.5 = (f32[1,512,1,512]{3,2,1,0:T(1,128)}, f32[1,512,1,512]{3,2,1,0:T(1,128)S(1)}, u32[]{:S(2)}, u32[]{:S(2)}) collective-permute-start(f32[1,512,1,512]{3,2,1,0:T(1,128)} %collective-permute-done.4.refs_2_), channel_id=1, source_target_pairs={{0,1},{1,0},{4,5},{5,4}} | collective-permute-start | bytes 3145736 | tf_op jit(solution)/shard_map/ppermute | solution.py:616
  30.2 1.7 collective-permute-start.1
  31.9 0.7 shard_map.29
  32.6 0.0 collective-permute-done.5.refs_3_
  32.6 1.0 copy-done.8
  33.6 9.4 %shard_map.30 = (f32[512,512]{1,0:T(8,128)}, f32[512,512]{1,0:T(8,128)}, f32[16,32,768]{2,1,0:T(8,128)}) custom-call(s32[4]{0:T(128)} %pad_add_fusion.refs_0_, f32[1,512,1,512]{3,2,1,0:T(1,128)} %refs_5_.3, f32[1,512,1,512]{3,2,1,0:T(1,128)} %collective-permute-done.4.refs_2_, f32[1,512,1,512]{3,2,1,0:T(1,128)} %copy-done.8, ...), custom_call_target="tpu_custom_call" | custom-call | tf_op jit(solution)/shard_map/pallas_call | solution.py:158
  43.0 0.6 all-to-all-done
  43.6 13.0 %all-to-all-start.1 = ((f32[16,32,768]{2,1,0:T(8,128)}), f32[16,32,768]{2,1,0:T(8,128)}, u32[]{:S(2)}, u32[]{:S(2)}) async-start(f32[16,32,768]{2,1,0:T(8,128)} %get-tuple-element.30), calls=%async_computation.1 | async-start | bytes 3145728 | tf_op jit(solution)/shard_map/all_to_all | solution.py:628
  56.6 0.7 collective-permute-start.2
  57.4 1.6 collective-permute-start.8
  59.0 0.1 reduce_sum.9.refs_4_
  59.1 0.0 copy-start.12
  59.1 4.4 %collective-permute-start.6 = (f32[32,768]{1,0:T(8,128)S(1)}, f32[32,768]{1,0:T(8,128)S(1)}, u32[]{:S(2)}, u32[]{:S(2)}) collective-permute-start(f32[32,768]{1,0:T(8,128)S(1)} %reduce_sum.9.refs_4_), channel_id=1, source_target_pairs={{0,16},{16,0},{1,17},{17,1},{2,18},{18,2},{3,19},{19,3},{4,20},{20... | collective-permute-start | bytes 294920 | tf_op jit(solution)/shard_map/ppermute | solution.py:624
  63.5 3.3 %collective-permute-done.6.refs_5_ = f32[32,768]{1,0:T(8,128)S(1)} collective-permute-done((f32[32,768]{1,0:T(8,128)S(1)}, f32[32,768]{1,0:T(8,128)S(1)}, u32[]{:S(2)}, u32[]{:S(2)}) %collective-permute-start.6) | collective-permute-done | bytes 98336 | tf_op jit(solution)/shard_map/ppermute | solution.py:624
  66.8 0.6 copy-done.14
  67.4 2.7 %shard_map.31 = f32[16,32,1024]{2,1,0:T(8,128)} custom-call(s32[4]{0:T(128)} %pad_add_fusion.refs_0_, f32[1,512,1,512]{3,2,1,0:T(1,128)} %collective-permute-done.1.refs_1_.refs_3_, f32[1,512,1,512]{3,2,1,0:T(1,128)} %copy-done.6, f32[1,512,1,512]{3,2,1,0:T(1,128)} %refs_5_.3, f32[32,768]{1,0:T(8,128)} %copy-done.12, f32[32,768]{1,0:T(8,128)} %copy-done.14), custom_call_target="tpu_custom_call" | custom-call | tf_op jit(solution)/shard_map/pallas_call | solution.py:158
  70.1 8.7 %all-to-all-done.1 = f32[16,32,768]{2,1,0:T(8,128)} async-done(((f32[16,32,768]{2,1,0:T(8,128)}), f32[16,32,768]{2,1,0:T(8,128)}, u32[]{:S(2)}, u32[]{:S(2)}) %all-to-all-start.1) | async-done | bytes 1572896 | tf_op jit(solution)/shard_map/all_to_all | solution.py:628
  78.8 5.6 %all-to-all-start.2 = ((f32[16,32,1024]{2,1,0:T(8,128)}), f32[16,32,1024]{2,1,0:T(8,128)S(1)}, u32[]{:S(2)}, u32[]{:S(2)}) async-start(f32[16,32,1024]{2,1,0:T(8,128)} %shard_map.31), calls=%async_computation.2 | async-start | bytes 4194304 | tf_op jit(solution)/shard_map/all_to_all | solution.py:628
  84.4 0.0 all-gather.2.cloned.1.call-start
  84.4 0.7 collective-permute-start.9
  85.2 0.9 slice_bitcast_fusion
  86.1 0.8 slice_bitcast_fusion.1
  86.9 1.3 collective-permute-start.7
  88.2 2.2 %collective-permute-done.7 = f32[32,1280]{1,0:T(8,128)S(1)} collective-permute-done((f32[32,1280]{1,0:T(8,128)S(1)}, f32[32,1280]{1,0:T(8,128)S(1)}, u32[]{:S(2)}, u32[]{:S(2)}) %collective-permute-start.7) | collective-permute-done | bytes 163872 | tf_op jit(solution)/shard_map/ppermute | solution.py:663
  90.5 0.7 fusion
  91.2 18.7 %all-to-all-done.2.refs_1_.refs_0_ = f32[16,32,1024]{2,1,0:T(8,128)S(1)} async-done(((f32[16,32,1024]{2,1,0:T(8,128)}), f32[16,32,1024]{2,1,0:T(8,128)S(1)}, u32[]{:S(2)}, u32[]{:S(2)}) %all-to-all-start.2) | async-done | bytes 2097184 | tf_op jit(solution)/shard_map/all_to_all | solution.py:628
  109.9 0.0 all-gather.2.cloned.1.call-update
  109.9 0.1 slice.15
  110.1 1.2 copy-done
  111.3 0.7 collective-permute-start.11
  112.1 1.2 copy-done.5
  113.3 0.8 shard_map.32
  114.0 0.7 collective-permute-start.14
  114.8 0.7 collective-permute-start.15
  115.5 2.4 %shard_map.35.refs_0_ = f32[32,1024]{1,0:T(8,128)} custom-call(f32[16,32,1024]{2,1,0:T(8,128)} %copy-done), custom_call_target="tpu_custom_call" | custom-call | tf_op jit(solution)/shard_map/pallas_call | solution.py:158
  117.8 1.3 collective-permute-start.18
  119.1 0.7 collective-permute-start.12
  119.9 0.8 copy-done.11
  120.7 0.8 shard_map.33
  121.5 1.3 collective-permute-start.16
  122.8 2.5 %collective-permute-done.18.refs_1_ = f32[32,1024]{1,0:T(8,128)S(1)} collective-permute-done((f32[32,1024]{1,0:T(8,128)}, f32[32,1024]{1,0:T(8,128)S(1)}, u32[]{:S(2)}, u32[]{:S(2)}) %collective-permute-start.18) | collective-permute-done | bytes 131104 | tf_op jit(solution)/shard_map/ppermute | solution.py:681
  125.3 0.6 copy-done.13
  125.9 2.6 %shard_map.36 = f32[16,32,1024]{2,1,0:T(8,128)} custom-call(f32[32,1024]{1,0:T(8,128)} %shard_map.35.refs_0_, f32[32,1024]{1,0:T(8,128)} %copy-done.13), custom_call_target="tpu_custom_call" | custom-call | tf_op jit(solution)/shard_map/pallas_call | solution.py:158
  128.5 5.7 %all-to-all-start.3 = ((f32[16,32,1024]{2,1,0:T(8,128)}), f32[16,32,1024]{2,1,0:T(8,128)S(1)}, u32[]{:S(2)}, u32[]{:S(2)}) async-start(f32[16,32,1024]{2,1,0:T(8,128)} %shard_map.36), calls=%async_computation.3 | async-start | bytes 4194304 | tf_op jit(solution)/shard_map/all_to_all | solution.py:628
  134.2 1.6 collective-permute-start.13
  135.8 51.7 %collective-permute-done.16.refs_11_ = f32[512,512]{1,0:T(8,128)} collective-permute-done((f32[512,512]{1,0:T(8,128)}, f32[512,512]{1,0:T(8,128)}, u32[]{:S(2)}, u32[]{:S(2)}) %collective-permute-start.16) | collective-permute-done | bytes 1048608 | tf_op jit(solution)/shard_map/ppermute | solution.py:616
  187.5 2.5 %collective-permute-start.17 = (f32[512,512]{1,0:T(8,128)}, f32[512,512]{1,0:T(8,128)}, u32[]{:S(2)}, u32[]{:S(2)}) collective-permute-start(f32[512,512]{1,0:T(8,128)} %collective-permute-done.16.refs_11_), channel_id=1, source_target_pairs={{0,1},{1,0}} | collective-permute-start | bytes 3145736 | tf_op jit(solution)/shard_map/ppermute | solution.py:616
  190.0 0.0 all-gather.2.cloned.1.call-done.refs_5_
  190.1 1.9 slice.16
  191.9 1.9 collective-permute-start.10
  193.9 0.9 shard_map.34.refs_14_
  194.9 1.2 collective-permute-done.10.refs_6_
  196.1 0.1 copy-done.4
  196.2 7.5 %shard_map.37 = f32[1,512,1,512]{3,2,1,0:T(1,128)} custom-call(s32[4]{0:T(128)} %pad_add_fusion.refs_0_, f32[1,512,1,512]{3,2,1,0:T(1,128)} %refs_1_.7, f32[1,512,1,512]{3,2,1,0:T(1,128)} %copy-done.3, f32[1,512,1,512]{3,2,1,0:T(1,128)} %collective-permute-done.1.refs_1_.refs_3_, f32[1,512,1,512]{3,2,1,0:T(1,128)} %copy-done.6, ...), custom_call_target="tpu_custom_call" | custom-call | tf_op jit(solution)/shard_map/pallas_call | solution.py:158
  (33 shorter events, 0.1 us)
Async XLA Ops:
  6.5 3.7 %collective-permute-start.3 = (f32[1,512,1,512]{3,2,1,0:T(1,128)}, f32[1,512,1,512]{3,2,1,0:T(1,128)S(1)}, u32[]{:S(2)}, u32[]{:S(2)}) collective-permute-start(f32[1,512,1,512]{3,2,1,0:T(1,128)} %refs_5_.3), channel_id=1, source_target_pairs={{2,3},{3,2},{6,7},{7,6},{10,11},{11,10},{14,15},{15,14},{18,19},{1... | collective-permute-start | bytes 3145736 | tf_op jit(solution)/shard_map/ppermute | solution.py:616
  7.3 3.0 %collective-permute-start = (f32[1,512,1,512]{3,2,1,0:T(1,128)}, f32[1,512,1,512]{3,2,1,0:T(1,128)S(1)}, u32[]{:S(2)}, u32[]{:S(2)}) collective-permute-start(f32[1,512,1,512]{3,2,1,0:T(1,128)} %refs_1_.7), channel_id=1, source_target_pairs={{2,3},{3,2},{6,7},{7,6},{10,11},{11,10},{14,15},{15,14},{18,19},{1... | collective-permute-start | bytes 3145736 | tf_op jit(solution)/shard_map/ppermute | solution.py:616
  8.0 15.0 %collective-permute-start.4 = (f32[1,512,1,512]{3,2,1,0:T(1,128)}, f32[1,512,1,512]{3,2,1,0:T(1,128)}, u32[]{:S(2)}, u32[]{:S(2)}) collective-permute-start(f32[1,512,1,512]{3,2,1,0:T(1,128)} %refs_5_.3), channel_id=1, source_target_pairs={{7,5},{2,0},{6,4}} | collective-permute-start | bytes 3145736 | tf_op jit(solution)/shard_map/ppermute | solution.py:616
  10.2 1.0 copy-start.1
  11.2 1.0 copy-start.3
  14.2 15.9 %copy-start.2 = (f32[1,512,1,512]{3,2,1,0:T(1,128)S(1)}, f32[1,512,1,512]{3,2,1,0:T(1,128)}, u32[]{:S(2)}) copy-start(f32[1,512,1,512]{3,2,1,0:T(1,128)} %refs_1_.7) | copy-start | bytes 3145732
  14.2 29.4 %all-to-all-start = ((f32[16,32,768]{2,1,0:T(8,128)}), f32[16,32,768]{2,1,0:T(8,128)S(1)}, u32[]{:S(2)}, u32[]{:S(2)}) async-start(f32[16,32,768]{2,1,0:T(8,128)} %shard_map.28), calls=%async_computation | async-start | bytes 3145728 | tf_op jit(solution)/shard_map/all_to_all | solution.py:628
  23.0 9.6 %collective-permute-start.5 = (f32[1,512,1,512]{3,2,1,0:T(1,128)}, f32[1,512,1,512]{3,2,1,0:T(1,128)S(1)}, u32[]{:S(2)}, u32[]{:S(2)}) collective-permute-start(f32[1,512,1,512]{3,2,1,0:T(1,128)} %collective-permute-done.4.refs_2_), channel_id=1, source_target_pairs={{0,1},{1,0},{4,5},{5,4}} | collective-permute-start | bytes 3145736 | tf_op jit(solution)/shard_map/ppermute | solution.py:616
  30.2 26.5 %collective-permute-start.1 = (f32[1,512,1,512]{3,2,1,0:T(1,128)S(1)}, f32[1,512,1,512]{3,2,1,0:T(1,128)}, u32[]{:S(2)}, u32[]{:S(2)}) collective-permute-start(f32[1,512,1,512]{3,2,1,0:T(1,128)S(1)} %copy-done.2), channel_id=1, source_target_pairs={{10,8},{11,9},{14,12},{15,13},{18,16},{19,17},{22,20},{23,21},{26,... | collective-permute-start | bytes 3145736 | tf_op jit(solution)/shard_map/ppermute | solution.py:616
  32.6 1.0 copy-start.8
  43.6 35.2 %all-to-all-start.1 = ((f32[16,32,768]{2,1,0:T(8,128)}), f32[16,32,768]{2,1,0:T(8,128)}, u32[]{:S(2)}, u32[]{:S(2)}) async-start(f32[16,32,768]{2,1,0:T(8,128)} %get-tuple-element.30), calls=%async_computation.1 | async-start | bytes 3145728 | tf_op jit(solution)/shard_map/all_to_all | solution.py:628
  56.6 6.9 %collective-permute-start.2 = (f32[1,512,1,512]{3,2,1,0:T(1,128)}, f32[1,512,1,512]{3,2,1,0:T(1,128)S(1)}, u32[]{:S(2)}, u32[]{:S(2)}) collective-permute-start(f32[1,512,1,512]{3,2,1,0:T(1,128)} %collective-permute-done.1.refs_1_.refs_3_), channel_id=1, source_target_pairs={{4,5},{5,4},{8,9},{9,8},{12,13},{13,12},{16,17},{17,16},{20,21},{2... | collective-permute-start | bytes 3145736 | tf_op jit(solution)/shard_map/ppermute | solution.py:616
  57.4 27.1 %collective-permute-start.8 = (f32[512,512]{1,0:T(8,128)}, f32[512,512]{1,0:T(8,128)}, u32[]{:S(2)}, u32[]{:S(2)}) collective-permute-start(f32[512,512]{1,0:T(8,128)} %get-tuple-element.27.refs_5_.refs_8_), channel_id=1, source_target_pairs={{6,2}} | collective-permute-start | bytes 3145736 | tf_op jit(solution)/shard_map/ppermute | solution.py:616
  59.1 7.7 %copy-start.12 = (f32[32,768]{1,0:T(8,128)}, f32[32,768]{1,0:T(8,128)S(1)}, u32[]{:S(2)}) copy-start(f32[32,768]{1,0:T(8,128)S(1)} %reduce_sum.9.refs_4_) | copy-start | bytes 294916
  59.1 7.7 %collective-permute-start.6 = (f32[32,768]{1,0:T(8,128)S(1)}, f32[32,768]{1,0:T(8,128)S(1)}, u32[]{:S(2)}, u32[]{:S(2)}) collective-permute-start(f32[32,768]{1,0:T(8,128)S(1)} %reduce_sum.9.refs_4_), channel_id=1, source_target_pairs={{0,16},{16,0},{1,17},{17,1},{2,18},{18,2},{3,19},{19,3},{4,20},{20... | collective-permute-start | bytes 294920 | tf_op jit(solution)/shard_map/ppermute | solution.py:624
  63.5 3.3 %copy-start.6 = (f32[1,512,1,512]{3,2,1,0:T(1,128)}, f32[1,512,1,512]{3,2,1,0:T(1,128)S(1)}, u32[]{:S(2)}) copy-start(f32[1,512,1,512]{3,2,1,0:T(1,128)S(1)} %collective-permute-done.2.refs_2_.refs_4_) | copy-start | bytes 3145732
  66.8 0.6 copy-start.14
  78.8 31.1 %all-to-all-start.2 = ((f32[16,32,1024]{2,1,0:T(8,128)}), f32[16,32,1024]{2,1,0:T(8,128)S(1)}, u32[]{:S(2)}, u32[]{:S(2)}) async-start(f32[16,32,1024]{2,1,0:T(8,128)} %shard_map.31), calls=%async_computation.2 | async-start | bytes 4194304 | tf_op jit(solution)/shard_map/all_to_all | solution.py:628
  84.4 105.7 %all-gather.2.cloned.1.call-start = ((), (), s32[]{:S(2)}) async-start(), calls=%async_computation.4 | async-start | bytes 2785280 | tf_op jit(solution)/shard_map/all_gather | solution.py:665
  84.4 6.7 %collective-permute-start.9 = (f32[512,512]{1,0:T(8,128)}, f32[512,512]{1,0:T(8,128)S(1)}, u32[]{:S(2)}, u32[]{:S(2)}) collective-permute-start(f32[512,512]{1,0:T(8,128)} %collective-permute-done.8.refs_8_), channel_id=1, source_target_pairs={{2,3}} | collective-permute-start | bytes 3145736 | tf_op jit(solution)/shard_map/ppermute | solution.py:616
  86.9 3.5 %collective-permute-start.7 = (f32[32,1280]{1,0:T(8,128)S(1)}, f32[32,1280]{1,0:T(8,128)S(1)}, u32[]{:S(2)}, u32[]{:S(2)}) collective-permute-start(f32[32,1280]{1,0:T(8,128)S(1)} %pad_maximum_fusion), channel_id=1, source_target_pairs={{0,16},{1,17},{2,18},{3,19},{4,20},{5,21},{6,22},{7,23},{8,24},{9,... | collective-permute-start | bytes 491528 | tf_op jit(solution)/shard_map/ppermute | solution.py:663
  91.2 18.9 %copy-start.7 = (f32[512,512]{1,0:T(8,128)}, f32[512,512]{1,0:T(8,128)S(1)}, u32[]{:S(2)}) copy-start(f32[512,512]{1,0:T(8,128)S(1)} %collective-permute-done.9.refs_9_) | copy-start | bytes 3145732
  109.9 1.4 copy-start
  111.3 0.8 collective-permute-start.11
  112.1 1.2 copy-start.5
  114.0 0.7 collective-permute-start.14
  114.8 5.1 %copy-start.10 = (f32[256,512]{1,0:T(8,128)}, f32[256,512]{1,0:T(8,128)S(1)}, u32[]{:S(2)}) copy-start(f32[256,512]{1,0:T(8,128)S(1)} %collective-permute-done.14.refs_10_) | copy-start | bytes 1572868
  114.8 5.1 %collective-permute-start.15 = (f32[256,512]{1,0:T(8,128)S(1)}, f32[256,512]{1,0:T(8,128)S(1)}, u32[]{:S(2)}, u32[]{:S(2)}) collective-permute-start(f32[256,512]{1,0:T(8,128)S(1)} %collective-permute-done.14.refs_10_), channel_id=1, source_target_pairs={{2,3},{3,2}} | collective-permute-start | bytes 1572872 | tf_op jit(solution)/shard_map/ppermute | solution.py:616
  117.8 7.4 %collective-permute-start.18 = (f32[32,1024]{1,0:T(8,128)}, f32[32,1024]{1,0:T(8,128)S(1)}, u32[]{:S(2)}, u32[]{:S(2)}) collective-permute-start(f32[32,1024]{1,0:T(8,128)} %shard_map.35.refs_0_), channel_id=1, source_target_pairs={{16,0},{17,1},{18,2},{19,3},{20,4},{21,5},{22,6},{23,7},{24,8},{25... | collective-permute-start | bytes 393224 | tf_op jit(solution)/shard_map/ppermute | solution.py:681
  119.1 15.0 %collective-permute-start.12 = (f32[512,512]{1,0:T(8,128)}, f32[512,512]{1,0:T(8,128)S(1)}, u32[]{:S(2)}, u32[]{:S(2)}) collective-permute-start(f32[512,512]{1,0:T(8,128)} %get-tuple-element.39), channel_id=1, source_target_pairs={{6,4},{7,5}} | collective-permute-start | bytes 3145736 | tf_op jit(solution)/shard_map/ppermute | solution.py:616
  119.9 0.8 copy-start.11
  121.5 66.0 %collective-permute-start.16 = (f32[512,512]{1,0:T(8,128)}, f32[512,512]{1,0:T(8,128)}, u32[]{:S(2)}, u32[]{:S(2)}) collective-permute-start(f32[512,512]{1,0:T(8,128)} %get-tuple-element.43), channel_id=1, source_target_pairs={{2,0},{3,1}} | collective-permute-start | bytes 3145736 | tf_op jit(solution)/shard_map/ppermute | solution.py:616
  125.3 0.6 copy-start.13
  128.5 66.3 %all-to-all-start.3 = ((f32[16,32,1024]{2,1,0:T(8,128)}), f32[16,32,1024]{2,1,0:T(8,128)S(1)}, u32[]{:S(2)}, u32[]{:S(2)}) async-start(f32[16,32,1024]{2,1,0:T(8,128)} %shard_map.36), calls=%async_computation.3 | async-start | bytes 4194304 | tf_op jit(solution)/shard_map/all_to_all | solution.py:628
  134.2 60.6 %copy-start.9 = (f32[512,512]{1,0:T(8,128)}, f32[512,512]{1,0:T(8,128)S(1)}, u32[]{:S(2)}) copy-start(f32[512,512]{1,0:T(8,128)S(1)} %collective-permute-done.12.refs_9_) | copy-start | bytes 3145732
  134.2 60.6 %collective-permute-start.13 = (f32[512,512]{1,0:T(8,128)S(1)}, f32[512,512]{1,0:T(8,128)}, u32[]{:S(2)}, u32[]{:S(2)}) collective-permute-start(f32[512,512]{1,0:T(8,128)S(1)} %collective-permute-done.12.refs_9_), channel_id=1, source_target_pairs={{4,5},{5,4}} | collective-permute-start | bytes 3145736 | tf_op jit(solution)/shard_map/ppermute | solution.py:616
  187.5 7.3 %collective-permute-start.17 = (f32[512,512]{1,0:T(8,128)}, f32[512,512]{1,0:T(8,128)}, u32[]{:S(2)}, u32[]{:S(2)}) collective-permute-start(f32[512,512]{1,0:T(8,128)} %collective-permute-done.16.refs_11_), channel_id=1, source_target_pairs={{0,1},{1,0}} | collective-permute-start | bytes 3145736 | tf_op jit(solution)/shard_map/ppermute | solution.py:616
  191.9 4.1 %collective-permute-start.10 = (f32[512,256]{1,0:T(8,128)}, f32[512,256]{1,0:T(8,128)}, u32[]{:S(2)}, u32[]{:S(2)}) collective-permute-start(f32[512,256]{1,0:T(8,128)} %slice.16), channel_id=1, source_target_pairs={{0,1},{1,0},{4,5},{5,4},{8,9},{9,8},{12,13},{13,12},{16,17},{17,16... | collective-permute-start | bytes 1572872 | tf_op jit(solution)/shard_map/ppermute | solution.py:616
  194.8 1.4 copy-start.4
Sparse Core Ops, SparseCore 0:
  110.1 63.4 all-gather.1

commit v3 on v2

--- a/solution.py
+++ b/solution.py
@@ -331,146 +331,229 @@
     out_ref[...] = jnp.broadcast_to(s[None], out_ref.shape)
 
 
-def gather_tile(bank, slot, core, got_ref, gotsw_ref, lo):
-    def begin(left, right):
-        for half, src in ((0, left), (H, right)):
-            for s in range(16):
-                pltpu.make_async_copy(
-                    src.at[s, :, lo:lo + H],
-                    bank.buf.at[slot, s * 32:(s + 1) * 32, half:half + H],
-                    bank.sem.at[slot]).start()
-
-    @pl.when(core == 0)
-    def _():
-        begin(got_ref, gotsw_ref)
-
-    @pl.when(core == 1)
-    def _():
-        begin(gotsw_ref, got_ref)
-
-
-def k_chain_a(pos_ref, got_ref, gotsw_ref, a_ref, asw_ref, l_ref, lsw_ref, i1_ref, x12_ref, sym_ref, ap_ref, out_ref, half_ref, buf, sem):
-    row, xl, core = pos_ref[0], pos_ref[1], pos_ref[2]
-    bank = Bank(buf, sem)
-    live = (xl == 1) & (row == 1)
-
-    @pl.when(live)
-    def _():
-        gather_tile(bank, 0, core, got_ref, gotsw_ref, 0)
+def join(bank, slot, core, here, there):
+    for c, (left, right) in enumerate(((0, H), (H, 0))):
+        @pl.when(core == c)
+        def _():
+            pltpu.make_async_copy(here, bank.buf.at[slot, :, left:left + H], bank.sem.at[slot]).start()
+            pltpu.make_async_copy(there, bank.buf.at[slot, :, right:right + H], bank.sem.at[slot]).start()
+
+
+def rows_of(bank, slot, src, lo, width):
+    for s in range(16):
+        pltpu.make_async_copy(
+            src.at[s, :, lo:lo + width], bank.buf.at[slot, s * 32:(s + 1) * 32, :width],
+            bank.sem.at[slot]).start()
+
+
+def tril_half(x, core):
+    i = lax.broadcasted_iota(jnp.int32, x.shape, 0)
+    j = lax.broadcasted_iota(jnp.int32, x.shape, 1) + core * H
+    return jnp.where(i >= j, x, 0.0)
+
+
+def k_one_p(pos_ref, got_ref, a_ref, asw_ref, l_ref, lsw_ref, i1_ref, p_ref, buf, sem):
+    row, xl, core = pos_ref[0], pos_ref[1], pos_ref[2]
+    bank = Bank(buf, sem)
+
+    @pl.when((xl == 1) & (row == 1))
+    def _():
+        rows_of(bank, 0, got_ref, 0, H)
         bank.start(1, i1_ref)
 
         @pl.when(core == 0)
         def _():
-            bank.start(2, asw_ref)
+            bank.start_half(2, asw_ref, 0)
             bank.start(3, lsw_ref)
-            bank.start(6, a_ref)
 
         @pl.when(core == 1)
         def _():
-            bank.start(2, a_ref)
+            bank.start_half(2, a_ref, H)
             bank.start(3, l_ref)
-            bank.start(6, asw_ref)
-
-        gather_tile(bank, 4, core, got_ref, gotsw_ref, H)
-        bank.start(5, x12_ref)
-        bank.wait(0, 1, 2, 3)
-        i1 = split(bank.get(1))
-        g = tril(bank.get(2) - mm(i1, bank.get(0), ta=True))
-        sym = sym_half(mm(tril(bank.get(3)), g, ta=True))
+
+        bank.wait_half(0)
+        bank.wait(1)
+        g = mm(bank.get(1), buf[0, :, :H], ta=True)
+        bank.wait_half(2)
+        g = tril_half(buf[2, :, :H] - g, core)
+        bank.wait(3)
+        p_ref[...] = mm(tril(bank.get(3)), g, ta=True)
+
+
+def k_one_w(pos_ref, got_ref, p_ref, psw_ref, a_ref, asw_ref, i1_ref, x12_ref, sym_ref, w_ref, ap_ref, buf, sem):
+    row, xl, core = pos_ref[0], pos_ref[1], pos_ref[2]
+    bank = Bank(buf, sem)
+
+    @pl.when((xl == 1) & (row == 1))
+    def _():
+        join(bank, 0, core, p_ref, psw_ref)
+        rows_of(bank, 1, got_ref, H, H)
+        bank.start(3, i1_ref)
+
+        @pl.when(core == 0)
+        def _():
+            bank.start_half(2, x12_ref, 0)
+            bank.start_half(4, a_ref, 0)
+
+        @pl.when(core == 1)
+        def _():
+            bank.start_half(2, x12_ref, H)
+            bank.start_half(4, asw_ref, H)
+
+        bank.wait(0)
+        sym = sym_half(bank.get(0))
         sym_ref[...] = sym
-        bank.wait(4, 5, 6)
-        inner = bank.get(4) + 2.0 * mm(sym, bank.get(5))
-        ap_ref[...] = bank.get(6) - mm(i1, inner, ta=True)
-        lo = pl.multiple_of(core * H, H)
-        buf[4] = inner
-        half_ref[...] = sym_ref[pl.ds(lo, H), :]
-        out_ref[:H, :] = half_ref[...]
-        out_ref[H:, :] = buf[4, pl.ds(lo, H), :]
-
-
-def k_chain_b(pos_ref, got_ref, gotsw_ref, a_ref, asw_ref, l_ref, lsw_ref, i2_ref, x12_ref, x12sw_ref, half_ref, halfsw_ref, sym_ref, out_ref, buf, sem):
-    row, xl, core = pos_ref[0], pos_ref[1], pos_ref[2]
-    bank = Bank(buf, sem)
-    live = (xl == 1) & (row == 0)
-
-    def stack(up, down):
-        pltpu.make_async_copy(up, buf.at[0, :H], sem.at[0]).start()
-        pltpu.make_async_copy(down, buf.at[0, H:], sem.at[0]).start()
-
-    @pl.when(live)
-    def _():
+        bank.wait_half(1, 2)
+        w = buf[1, :, :H] + 2.0 * mm(sym, buf[2, :, :H])
+        w_ref[...] = w
+        bank.wait(3)
+        bank.wait_half(4)
+        ap_ref[...] = buf[4, :, :H] - mm(bank.get(3), w, ta=True)
+
+
+def k_zero_base(pos_ref, got_ref, t12_ref, t12sw_ref, a_ref, asw_ref, i2_ref, x12_ref, x12sw_ref, base_ref, buf, sem):
+    row, xl, core = pos_ref[0], pos_ref[1], pos_ref[2]
+    bank = Bank(buf, sem)
+
+    @pl.when((xl == 1) & (row == 0))
+    def _():
+        for c, (left, right) in enumerate(((t12_ref, t12sw_ref), (t12sw_ref, t12_ref))):
+            @pl.when(core == c)
+            def _():
+                for s in range(16):
+                    at = pl.ds(s * 32, 32)
+                    pltpu.make_async_copy(left.at[s], buf.at[0, at, :H], sem.at[0]).start()
+                    pltpu.make_async_copy(right.at[s], buf.at[0, at, H:], sem.at[0]).start()
+
+        rows_of(bank, 2, got_ref, N, H)
+        bank.start(3, i2_ref)
+
         @pl.when(core == 0)
         def _():
-            stack(half_ref, halfsw_ref)
+            bank.start_half(1, x12_ref, 0)
+            bank.start_half(4, a_ref, 0)
+
+        @pl.when(core == 1)
+        def _():
+            bank.start_half(1, x12sw_ref, H)
+            bank.start_half(4, asw_ref, H)
+
+        bank.wait(0)
+        bank.wait_half(1)
+        inner = mm(bank.get(0), buf[1, :, :H], ta=True)
+        bank.wait_half(2)
+        bank.wait(3)
+        inner = mm(bank.get(3), buf[2, :, :H] - inner, ta=True)
+        bank.wait_half(4)
+        base_ref[...] = buf[4, :, :H] - inner
+
+
+def k_zero_w(pos_ref, got_ref, p_ref, psw_ref, x12_ref, x12sw_ref, w_ref, buf, sem):
+    row, xl, core = pos_ref[0], pos_ref[1], pos_ref[2]
+    bank = Bank(buf, sem)
+
+    @pl.when((xl == 1) & (row == 0))
+    def _():
+        join(bank, 0, core, p_ref, psw_ref)
+        rows_of(bank, 1, got_ref, H, H)
+
+        @pl.when(core == 0)
+        def _():
+            bank.start_half(2, x12_ref, 0)
+
+        @pl.when(core == 1)
+        def _():
+            bank.start_half(2, x12sw_ref, H)
+
+        bank.wait(0)
+        sym = sym_half(bank.get(0))
+        bank.wait_half(1, 2)
+        w_ref[...] = buf[1, :, :H] + 2.0 * mm(sym, buf[2, :, :H])
+
+
+def k_zero_p(pos_ref, base_ref, w_ref, x12_ref, x12sw_ref, i2_ref, l_ref, lsw_ref, p_ref, buf, sem):
+    row, xl, core = pos_ref[0], pos_ref[1], pos_ref[2]
+    bank = Bank(buf, sem)
+
+    @pl.when((xl == 1) & (row == 0))
+    def _():
+        bank.start_half(0, w_ref, 0)
+
+        @pl.when(core == 0)
+        def _():
             bank.start(1, x12_ref)
+            bank.start(3, l_ref)
 
         @pl.when(core == 1)
         def _():
-            stack(halfsw_ref, half_ref)
             bank.start(1, x12sw_ref)
-
-        gather_tile(bank, 2, core, got_ref, gotsw_ref, H)
-        gather_tile(bank, 3, core, got_ref, gotsw_ref, N)
-        bank.start(4, i2_ref)
-
-        @pl.when(core == 0)
-        def _():
-            bank.start(5, a_ref)
-            bank.start(6, l_ref)
-
-        @pl.when(core == 1)
-        def _():
-            bank.start(5, asw_ref)
-            bank.start(6, lsw_ref)
-
-        bank.wait(0, 1, 2)
-        x12 = split(bank.get(1))
-        buf[7] = bank.get(2) + 2.0 * mm(bank.get(0), x12)
-        inner = mm(x12, bank.get(7), ta=True) + mm(bank.get(2), x12, ta=True)
-        bank.wait(3, 4, 5, 6)
-        g = tril(bank.get(5) - mm(bank.get(4), bank.get(3) - inner, ta=True))
-        sym_ref[...] = sym_half(mm(tril(bank.get(6)), g, ta=True))
-        lo = pl.multiple_of(core * H, H)
-        out_ref[:H, :] = sym_ref[pl.ds(lo, H), :]
-        out_ref[H:, :] = buf[7, pl.ds(lo, H), :]
-
-
-def k_chain_c(pos_ref, sym1_ref, sym2_ref, inv_ref, e_ref, buf, sem):
+            bank.start(3, lsw_ref)
+
+        bank.start(2, i2_ref)
+        bank.start_half(4, base_ref, 0)
+        bank.wait_half(0)
+        bank.wait(1)
+        inner = mm(bank.get(1), buf[0, :, :H], ta=True)
+        bank.wait(2)
+        inner = mm(bank.get(2), inner, ta=True)
+        bank.wait_half(4)
+        g = tril_half(buf[4, :, :H] + inner, core)
+        bank.wait(3)
+        p_ref[...] = mm(tril(bank.get(3)), g, ta=True)
+
+
+def k_ends(pos_ref, sym1_ref, p_ref, psw_ref, inv_ref, e_ref, buf, sem):
     row, xl, core = pos_ref[0], pos_ref[1], pos_ref[2]
     bank = Bank(buf, sem)
 
     @pl.when((xl == 1) & (row == 0) & (core == 0))
     def _():
-        bank.start(0, sym2_ref)
+        join(bank, 0, core, p_ref, psw_ref)
+        bank.wait(0)
+        buf[0] = sym_half(buf[0])
 
     @pl.when((xl == 1) & (row == 1) & (core == 1))
     def _():
         bank.start(0, sym1_ref)
+        bank.wait(0)
 
     @pl.when((xl == 1) & (((row == 1) & (core == 1)) | ((row == 0) & (core == 0))))
     def _():
         bank.start(1, inv_ref)
-        bank.wait(0, 1)
+        bank.wait(1)
         inv = split(bank.get(1))
         e_ref[...] = mm(inv, mm(bank.get(0), inv), ta=True)
 
 
-def k_final(pos_ref, a_ref, asw_ref, ac_ref, acsw_ref, xs_ref, xh_ref, inv_ref, x_ref, one_ref, onesw_ref, zero_ref, zerosw_ref, ap_ref, e_ref, *rest):
-    ts_ref, res, buf, sem = rest
+def even_zero(row, xl, core):
+    return (xl == 0) & (row == 0)
+
+
+def k_before(pos_ref, xs_ref, xh_ref, ts_ref, w_ref, wsw_ref, out_ref, buf, sem):
+    row, xl, core = pos_ref[0], pos_ref[1], pos_ref[2]
+    bank = Bank(buf, sem)
+
+    @pl.when((xl == 0) & (row == 0))
+    def _():
+        rows_of(bank, 0, ts_ref, 0, N)
+        join(bank, 1, core, xs_ref.at[:, 2 * N:], xh_ref)
+        join(bank, 2, core, w_ref, wsw_ref)
+        bank.start(3, xs_ref.at[:, N:2 * N])
+        rows_of(bank, 4, ts_ref, N, N)
+        bank.wait(0, 1)
+        inner = mm(bank.get(1), bank.get(0), ta=True)
+        bank.wait(2, 3)
+        inner = inner + mm(bank.get(2), bank.get(3), ta=True)
+        bank.wait(4)
+        out_ref[...] = bank.get(4) - inner
+
+
+def k_final(pos_ref, a_ref, asw_ref, ac_ref, acsw_ref, xs_ref, xh_ref, ts_ref, inv_ref, x_ref, one_ref, onesw_ref, w_ref, wsw_ref, pre_ref, p_ref, psw_ref, ap_ref, apsw_ref, e_ref, res, buf, sem):
     row, xl, core = pos_ref[0], pos_ref[1], pos_ref[2]
     bank = Bank(buf, sem)
     X1, X2, X12, A, A3, A2 = 0, 1, 2, 3, 4, 5
     SYM, W, T, INV, XOWN, L1 = 2, 4, 5, 6, 7, 8
 
-    def rows_of(slot, src, lo, width):
-        for s in range(16):
-            pltpu.make_async_copy(
-                src.at[s, :, lo:lo + width], bank.buf.at[slot, s * 32:(s + 1) * 32, :width],
-                bank.sem.at[slot]).start()
-
-    def sums(slot, lo):
-        rows_of(slot, ts_ref, lo, N)
-
     def x2(slot):
         bank.start(slot, xs_ref.at[:, :N])
 
@@ -478,22 +561,7 @@
         bank.start(slot, xs_ref.at[:, N:2 * N])
 
     def x12(slot):
-        for c, (left, right) in enumerate(((0, H), (H, 0))):
-            @pl.when(core == c)
-            def _():
-                pltpu.make_async_copy(
-                    xs_ref.at[:, 2 * N:], bank.buf.at[slot, :, left:left + H], bank.sem.at[slot]).start()
-                pltpu.make_async_copy(
-                    xh_ref, bank.buf.at[slot, :, right:right + H], bank.sem.at[slot]).start()
-
-    def stack(slot, lo, here, there):
-        for c, (up, down) in enumerate(((here, there), (there, here))):
-            @pl.when(core == c)
-            def _():
-                pltpu.make_async_copy(
-                    up.at[lo:lo + H], bank.buf.at[slot, :H], bank.sem.at[slot]).start()
-                pltpu.make_async_copy(
-                    down.at[lo:lo + H], bank.buf.at[slot, H:], bank.sem.at[slot]).start()
+        join(bank, slot, core, xs_ref.at[:, 2 * N:], xh_ref)
 
     low_even = (row >= 2) & (xl == 0)
 
@@ -551,11 +619,11 @@
         def _():
             bank.start(L1, acsw_ref)
 
-        stack(W, H, one_ref, onesw_ref)
+        join(bank, W, core, w_ref, wsw_ref)
         x2(X2)
-        stack(SYM, 0, one_ref, onesw_ref)
+        join(bank, SYM, core, one_ref, onesw_ref)
         bank.start(XOWN, x_ref)
-        sums(T, 0)
+        rows_of(bank, T, ts_ref, 0, N)
         bank.start(A, a_ref)
         bank.wait(INV, L1, W)
         inv = split(bank.get(INV))
@@ -563,33 +631,25 @@
         bank.wait(X2)
         side = mm(ap, bank.get(X2))
         bank.wait(SYM, XOWN)
-        inner = 2.0 * mm(bank.get(SYM), bank.get(XOWN))
+        inner = 2.0 * mm(sym_half(bank.get(SYM)), bank.get(XOWN))
         bank.wait(T, A)
         res[...] = bank.get(A) - side - mm(inv, inner + bank.get(T), ta=True)
 
     @pl.when((row == 0) & (xl == 0))
     def _():
-        sums(T, 0)
-        x12(L1)
-        stack(W, H, zero_ref, zerosw_ref)
-        x1(X1)
-        stack(SYM, 0, zero_ref, zerosw_ref)
+        join(bank, SYM, core, p_ref, psw_ref)
         bank.start(XOWN, x_ref)
-        sums(X2, N)
+        bank.start(T, pre_ref)
         bank.start(INV, inv_ref)
         bank.start(A, a_ref)
-        bank.wait(T, L1)
-        inner = -mm(bank.get(L1), bank.get(T), ta=True)
-        bank.wait(W, X1)
-        inner = inner - mm(bank.get(W), bank.get(X1), ta=True)
         bank.wait(SYM, XOWN)
-        inner = inner + 2.0 * mm(bank.get(SYM), bank.get(XOWN))
-        bank.wait(X2, INV, A)
-        res[...] = bank.get(A) - mm(bank.get(INV), inner + bank.get(X2), ta=True)
+        inner = 2.0 * mm(sym_half(bank.get(SYM)), bank.get(XOWN))
+        bank.wait(T, INV, A)
+        res[...] = bank.get(A) - mm(bank.get(INV), inner + bank.get(T), ta=True)
 
     @pl.when((row == 1) & (xl == 1) & (core == 0))
     def _():
-        bank.start(A, ap_ref)
+        join(bank, A, core, ap_ref, apsw_ref)
         x2(X2)
         bank.wait(A, X2)
         res[...] = mm(bank.get(A), bank.get(X2))
@@ -634,60 +694,81 @@
     y, xh, z = (lax.axis_index(n) for n in ("y", "xh", "z"))
     xl, core = lax.axis_index("xl"), lax.axis_index("core")
     pos = jnp.stack([y * 8 + xh * 4 + z, xl, core, z]).astype(jnp.int32)
-    tile = (N, N)
+    tile, half = (N, N), (N, H)
+    after = lax.optimization_barrier
 
     adj_sw = exchange_cores(adj, rows, (2, 3))
     low_sw = exchange_cores(low, rows, (2, 3))
     kq = move(low, [((1, 3), (1, 1)), ((0, 2), (0, 0)), ((1, 2), (1, 0))])
-    ac = move(adj, [((r, c), (r, c - 2)) for r in below for c in (2, 3)] + [((1, 2), (1, 0))])
 
     sums_odd, = call(k_sum_odd, [(16, 32, N + H)], pos, adj, adj_sw, low, low_sw, slots=4)
     got = every(sums_odd)
+    ac = move(adj, [((r, c), (r, c - 2)) for r in below for c in (2, 3)] + [((1, 2), (1, 0))])
 
     inv_odd, x12 = call(k_first, [tile, tile], pos, low, low_sw, slots=2, only=odd_top)
+    kq, inv_odd = after((kq, inv_odd))
     kq_sw = exchange_cores(kq, (0, 1), (0, 1))
     inv, x, send_x = call(
         k_second, [tile, tile, (16, 32, N + H)], pos, low, kq, kq_sw, inv_odd, x12, slots=3)
     x12_zero = move(x12, [((1, 2), (0, 2))])
     x12_zero_sw = exchange_cores(x12_zero, (0,), (2,))
-    got, send_x = lax.optimization_barrier((got, send_x))
+    got, send_x = after((got, send_x))
     got_x = every(send_x)
 
     part = jnp.sum(got, axis=0)
     other = swap_xh(part)
+    ac, send_x = after((ac, send_x))
     ac_sw = exchange_cores(ac, range(1, 32), (0, 1))
     send, = call(k_send, [(16, 32, 2 * N)], pos, ac, ac_sw, low, part, other, slots=3, near=(4, 5))
-    send, got_x = lax.optimization_barrier((send, got_x))
+    send, got_x = after((send, got_x))
     sums = every(send)
     xs = jnp.concatenate([got_x[0, :, :N], got_x[1]], 1)
     xs = xs + lax.ppermute(xs, "xh", [(0, 1)])
-    sums, xs, x12_zero_sw = lax.optimization_barrier((sums, xs, x12_zero_sw))
+    sums, xs, x12_zero_sw = after((sums, xs, x12_zero_sw))
     xs = lax.all_gather(xs, PLANE, tiled=True)
-    sums_sw = exchange_cores(sums[:, :, :N + H], (0, 1), (2, 3))
-    sym1, ap, to_one, half = call(
-        k_chain_a, [tile, tile, tile, (H, N)], pos, sums, sums_sw, adj, adj_sw, low, low_sw, inv_odd, x12,
-        slots=7, only=odd_one)
-    sums, to_one, half = lax.optimization_barrier((sums, to_one, half))
-    half = move(half, [((1, c), (0, c)) for c in (2, 3)])
-    one = move(to_one, [((1, 2), (1, 0)), ((1, 3), (1, 1))])
-    half_sw = exchange_cores(half, (0,), (2, 3))
-    sym2, to_zero = call(
-        k_chain_b, [tile, tile], pos, sums, sums_sw, adj, adj_sw, low, low_sw, inv_odd, x12_zero, x12_zero_sw,
-        half, half_sw, slots=8, only=odd_zero)
-    zero = move(to_zero, [((0, 2), (0, 0)), ((0, 3), (0, 1))])
-
-    own, = call(k_own, [(32, 2 * N)], sums, near=(0,))
+
+    p1, = call(k_one_p, [half], pos, sums, adj, adj_sw, low, low_sw, inv_odd, slots=4, only=odd_one)
+    p1_zero = move(p1, [((1, c), (0, c)) for c in (2, 3)])
+    p1_one = move(p1, [((1, 2), (1, 0)), ((1, 3), (1, 1))])
+    p1_sw = exchange_cores(p1, (1,), (2, 3))
+
+    sums_own, p1 = after((sums, p1))
+    own, = call(k_own, [(32, 2 * N)], sums_own, near=(0,))
     send, = call(
         k_spread, [(16, 32, 2 * N)], own, lax.ppermute(own, "xh", [(1, 0)]), near=(0, 1))
     ts = every(send)
 
-    e, = call(k_chain_c, [tile], pos, sym1, sym2, inv_odd, slots=2, only=odd_top)
-    one_sw = exchange_cores(one, (1,), (0, 1))
-    zero_sw = exchange_cores(zero, (0,), (0, 1))
+    t12 = sums[:, :, H:N]
+    t12_sw = exchange_cores(t12, (0,), (2, 3))
+    base, = call(
+        k_zero_base, [half], pos, sums, t12, t12_sw, adj, adj_sw, inv_odd, x12_zero, x12_zero_sw,
+        slots=5, only=odd_zero)
+    sym1, w1, ap = call(
+        k_one_w, [tile, half, half], pos, sums, p1, p1_sw, adj, adj_sw, inv_odd, x12, slots=5, only=odd_one)
+    w_one = move(w1, [((1, 2), (1, 0)), ((1, 3), (1, 1))])
+
+    p1_zero, base, send = after((p1_zero, base, send))
+    p1_zero_sw = exchange_cores(p1_zero, (0,), (2, 3))
+    w0, = call(
+        k_zero_w, [half], pos, sums, p1_zero, p1_zero_sw, x12_zero, x12_zero_sw, slots=3, only=odd_zero)
+    w_zero = move(w0, [((0, 2), (0, 0)), ((0, 3), (0, 1))])
+    p2, = call(
+        k_zero_p, [half], pos, base, w0, x12_zero, x12_zero_sw, inv_odd, low, low_sw, slots=5, only=odd_zero)
+    p2_zero = move(p2, [((0, 2), (0, 0)), ((0, 3), (0, 1))])
+    p2_sw = exchange_cores(p2, (0,), (3,))
+    ap_sw = exchange_cores(ap, (1,), (3,))
+    e, = call(k_ends, [tile], pos, sym1, p2, p2_sw, inv_odd, slots=2, only=odd_top)
+
+    p1_one_sw = exchange_cores(p1_one, (1,), (0, 1))
+    w_one_sw = exchange_cores(w_one, (1,), (0, 1))
+    w_zero_sw = exchange_cores(w_zero, (0,), (0, 1))
     xs_sw = exchange_cores(xs[:, 2 * N:], rows, (0, 1))
+    pre, = call(
+        k_before, [tile], pos, xs, xs_sw, ts, w_zero, w_zero_sw, slots=5, only=even_zero)
+    p2_zero_sw = exchange_cores(p2_zero, (0,), (0, 1))
     out, = call(
-        k_final, [adj.shape], pos, adj, adj_sw, ac, ac_sw, xs, xs_sw, inv, x,
-        one, one_sw, zero, zero_sw, ap, e, ts, slots=9)
+        k_final, [adj.shape], pos, adj, adj_sw, ac, ac_sw, xs, xs_sw, ts, inv, x,
+        p1_one, p1_one_sw, w_one, w_one_sw, pre, p2_zero, p2_zero_sw, ap, ap_sw, e, slots=9)
     return out
 
 

time: 214 us -> 206 us (0.963); the launches traced: 211 us -> 205 us
  waiting for transfers between devices: 89 us -> 66 us
  starting transfers between devices: 65.3 us -> 76.3 us
  Pallas kernels: 29.8 us -> 35.3 us
    ppermute x16 -> x23, waiting for transfers between devices: 53 us -> 21.5 us  [move(): return lax.ppermute(x, ALL, [(dev(*a), dev(*b)) for a, b in pairs])]
    ppermute x16 -> x23, starting transfers between devices: 25.2 us -> 36.4 us  [move(): return lax.ppermute(x, ALL, [(dev(*a), dev(*b)) for a, b in pairs])]
    all_gather x1, waiting for transfers between devices: 0.02 us -> 5.83 us  [local(): xs = lax.all_gather(xs, PLANE, tiled=True)]
    pallas_call x10 -> x14, Pallas kernels: 29.8 us -> 35.3 us  [call(): pl.pallas_call(body, out_shape=[jax.ShapeDtypeStruct(s, F32) for s in out...]
    ppermute x1, waiting for transfers between devices: 2.5 us -> 6.13 us  [local(): lax.ppermute(own, 'xh', [(1, 0)])]
    unnamed x30 -> x34, local copies, waits for them, and re-layouts: 7.48 us -> 8.62 us
  transfers between devices with their start and end apart: 24 -> 31, of which waited for: 8 -> 9; matrix products, arithmetic and copies ran while one was open for 2% -> 2% of each run, Pallas kernels for 11% -> 15%
where the time goes in v3:
time: 206 us; the launch traced here: 205 us
  starting transfers between devices  76.3 us (37%)
  waiting for transfers between devices  66 us (32%)
  Pallas kernels  35.3 us (17%)
  between operations  13.9 us (7%)
  local copies, waits for them, and re-layouts  12.3 us (6%)
    ppermute x23, starting transfers between devices, move(): return lax.ppermute(x, ALL, [(dev(*a), dev(*b)) for a, b in pairs])  36.4 us
    pallas_call x14, Pallas kernels, call(): pl.pallas_call(body, out_shape=[jax.ShapeDtypeStruct(s, F32) for s in out...  35.3 us
    all_to_all x4, starting transfers between devices, every(): return lax.all_to_all(x, PLANE, 0, 0, tiled=True)  32.9 us
    all_to_all x4, waiting for transfers between devices, every(): return lax.all_to_all(x, PLANE, 0, 0, tiled=True)  27.1 us
    ppermute x23, waiting for transfers between devices, move(): return lax.ppermute(x, ALL, [(dev(*a), dev(*b)) for a, b in pairs])  21.5 us
    unnamed x34, local copies, waits for them, and re-layouts  8.62 us
    ppermute x1, waiting for transfers between devices, local(): lax.ppermute(own, 'xh', [(1, 0)])  6.13 us
    all_gather x1, waiting for transfers between devices, local(): xs = lax.all_gather(xs, PLANE, tiled=True)  5.83 us
  transfers between devices with their start and end apart: 31, of which 9 were waited for; matrix products, arithmetic and copies ran while one was open for 2% of the time, Pallas kernels for 15%

profile of v3, /device:TPU:1, one launch (start us, length us, event | category | flops | bytes accessed | tf_op | source)
XLA Modules:
  0.0 205.2 jit_solution(6744394210060353508)
XLA Ops:
  6.5 0.7 collective-permute-start.2
  7.3 0.7 collective-permute-start
  8.0 1.7 collective-permute-start.3
  10.3 1.0 copy-done.4
  11.3 1.1 copy-done.2
  12.3 2.0 shard_map.28
  14.3 8.6 %all-to-all-start = ((f32[16,32,768]{2,1,0:T(8,128)}), f32[16,32,768]{2,1,0:T(8,128)S(1)}, u32[]{:S(2)}, u32[]{:S(2)}) async-start(f32[16,32,768]{2,1,0:T(8,128)} %shard_map.28), calls=%async_computation | async-start | bytes 3145728 | tf_op jit(solution)/shard_map/all_to_all | solution.py:688
  23.0 0.9 shard_map.29
  23.9 6.3 %collective-permute-start.4 = (f32[1,512,1,512]{3,2,1,0:T(1,128)}, f32[1,512,1,512]{3,2,1,0:T(1,128)S(1)}, u32[]{:S(2)}, u32[]{:S(2)}) collective-permute-start(f32[1,512,1,512]{3,2,1,0:T(1,128)} %collective-permute-done.3.refs_2_), channel_id=1, source_target_pairs={{0,1},{1,0},{4,5},{5,4}} | collective-permute-start | bytes 3145736 | tf_op jit(solution)/shard_map/ppermute | solution.py:676
  30.2 1.7 collective-permute-start.1
  31.9 0.7 collective-permute-done.4.refs_3_
  32.6 1.0 copy-done.9
  33.6 9.4 %shard_map.30 = (f32[512,512]{1,0:T(8,128)}, f32[512,512]{1,0:T(8,128)}, f32[16,32,768]{2,1,0:T(8,128)}) custom-call(s32[4]{0:T(128)} %pad_add_fusion.refs_0_, f32[1,512,1,512]{3,2,1,0:T(1,128)} %refs_6_.1, f32[1,512,1,512]{3,2,1,0:T(1,128)} %collective-permute-done.3.refs_2_, f32[1,512,1,512]{3,2,1,0:T(1,128)} %copy-done.9, ...), custom_call_target="tpu_custom_call" | custom-call | tf_op jit(solution)/shard_map/pallas_call | solution.py:158
  43.6 13.0 %all-to-all-start.1 = ((f32[16,32,768]{2,1,0:T(8,128)}), f32[16,32,768]{2,1,0:T(8,128)}, u32[]{:S(2)}, u32[]{:S(2)}) async-start(f32[16,32,768]{2,1,0:T(8,128)} %get-tuple-element.32), calls=%async_computation.1 | async-start | bytes 3145728 | tf_op jit(solution)/shard_map/all_to_all | solution.py:688
  56.6 1.7 collective-permute-start.5
  58.3 0.7 collective-permute-start.8
  59.1 4.4 %collective-permute-start.6 = (f32[32,768]{1,0:T(8,128)S(1)}, f32[32,768]{1,0:T(8,128)S(1)}, u32[]{:S(2)}, u32[]{:S(2)}) collective-permute-start(f32[32,768]{1,0:T(8,128)S(1)} %reduce_sum.9.refs_4_), channel_id=1, source_target_pairs={{0,16},{16,0},{1,17},{17,1},{2,18},{18,2},{3,19},{19,3},{4,20},{20... | collective-permute-start | bytes 294920 | tf_op jit(solution)/shard_map/ppermute | solution.py:684
  63.5 3.3 %collective-permute-done.6.refs_5_ = f32[32,768]{1,0:T(8,128)S(1)} collective-permute-done((f32[32,768]{1,0:T(8,128)S(1)}, f32[32,768]{1,0:T(8,128)S(1)}, u32[]{:S(2)}, u32[]{:S(2)}) %collective-permute-start.6) | collective-permute-done | bytes 98336 | tf_op jit(solution)/shard_map/ppermute | solution.py:684
  67.4 2.7 %shard_map.31 = f32[16,32,1024]{2,1,0:T(8,128)} custom-call(s32[4]{0:T(128)} %pad_add_fusion.refs_0_, f32[1,512,1,512]{3,2,1,0:T(1,128)} %collective-permute-done.1.refs_1_.refs_3_, f32[1,512,1,512]{3,2,1,0:T(1,128)} %collective-permute-done.5.refs_2_.refs_4_, f32[1,512,1,512]{3,2,1,0:T(1,128)} %refs_6_.1, f32[32,768]{1,0:T(8,128)} %copy-done.14, ...), custom_call_target="tpu_custom_call" | custom-call | tf_op jit(solution)/shard_map/pallas_call | solution.py:158
  70.1 8.7 %all-to-all-done.1 = f32[16,32,768]{2,1,0:T(8,128)} async-done(((f32[16,32,768]{2,1,0:T(8,128)}), f32[16,32,768]{2,1,0:T(8,128)}, u32[]{:S(2)}, u32[]{:S(2)}) %all-to-all-start.1) | async-done | bytes 1572896 | tf_op jit(solution)/shard_map/all_to_all | solution.py:688
  78.8 5.6 %all-to-all-start.2 = ((f32[16,32,1024]{2,1,0:T(8,128)}), f32[16,32,1024]{2,1,0:T(8,128)S(1)}, u32[]{:S(2)}, u32[]{:S(2)}) async-start(f32[16,32,1024]{2,1,0:T(8,128)} %shard_map.31), calls=%async_computation.2 | async-start | bytes 4194304 | tf_op jit(solution)/shard_map/all_to_all | solution.py:688
  84.4 1.7 collective-permute-start.9
  86.1 0.9 slice_bitcast_fusion
  87.0 0.8 slice_bitcast_fusion.1
  87.8 1.3 collective-permute-start.7
  89.1 2.2 %collective-permute-done.7 = f32[32,1280]{1,0:T(8,128)S(1)} collective-permute-done((f32[32,1280]{1,0:T(8,128)S(1)}, f32[32,1280]{1,0:T(8,128)S(1)}, u32[]{:S(2)}, u32[]{:S(2)}) %collective-permute-start.7) | collective-permute-done | bytes 163872 | tf_op jit(solution)/shard_map/ppermute | solution.py:726
  91.4 0.7 fusion
  92.1 17.8 %all-to-all-done.2.refs_1_.refs_0_ = f32[16,32,1024]{2,1,0:T(8,128)S(1)} async-done(((f32[16,32,1024]{2,1,0:T(8,128)}), f32[16,32,1024]{2,1,0:T(8,128)S(1)}, u32[]{:S(2)}, u32[]{:S(2)}) %all-to-all-start.2) | async-done | bytes 2097184 | tf_op jit(solution)/shard_map/all_to_all | solution.py:688
  110.0 0.7 collective-permute-start.18
  111.2 0.7 shard_map.32.refs_2_
  112.0 0.7 collective-permute-start.17
  112.7 2.4 %shard_map.33.refs_0_ = f32[32,1024]{1,0:T(8,128)} custom-call(f32[16,32,1024]{2,1,0:T(8,128)} %copy-done), custom_call_target="tpu_custom_call" | custom-call | tf_op jit(solution)/shard_map/pallas_call | solution.py:158
  115.1 1.3 collective-permute-start.11
  116.4 6.1 %collective-permute-done.11.refs_1_ = f32[32,1024]{1,0:T(8,128)S(1)} collective-permute-done((f32[32,1024]{1,0:T(8,128)}, f32[32,1024]{1,0:T(8,128)S(1)}, u32[]{:S(2)}, u32[]{:S(2)}) %collective-permute-start.11) | collective-permute-done | bytes 131104 | tf_op jit(solution)/shard_map/ppermute | solution.py:738
  122.5 0.6 copy-done.15
  123.1 2.5 %shard_map.34 = f32[16,32,1024]{2,1,0:T(8,128)} custom-call(f32[32,1024]{1,0:T(8,128)} %shard_map.33.refs_0_, f32[32,1024]{1,0:T(8,128)} %copy-done.15), custom_call_target="tpu_custom_call" | custom-call | tf_op jit(solution)/shard_map/pallas_call | solution.py:158
  125.7 0.8 copy-done.12
  126.5 0.7 shard_map.36.refs_1_
  127.3 1.6 collective-permute-start.19
  128.9 5.7 %all-to-all-start.3 = ((f32[16,32,1024]{2,1,0:T(8,128)}), f32[16,32,1024]{2,1,0:T(8,128)S(1)}, u32[]{:S(2)}, u32[]{:S(2)}) async-start(f32[16,32,1024]{2,1,0:T(8,128)} %shard_map.34), calls=%async_computation.3 | async-start | bytes 4194304 | tf_op jit(solution)/shard_map/all_to_all | solution.py:688
  134.6 0.7 collective-permute-start.14
  135.3 0.7 shard_map.37.refs_2_
  136.0 1.3 collective-permute-start.20
  137.3 0.7 collective-permute-start.12
  138.0 0.8 copy-done.13
  138.8 0.8 shard_map.35
  139.6 1.5 collective-permute-start.15
  141.1 0.7 shard_map.39.refs_2_
  141.8 1.5 collective-permute-start.25
  143.3 1.3 collective-permute-start.22
  144.6 20.7 %collective-permute-done.20.refs_4_ = f32[512,256]{1,0:T(8,128)} collective-permute-done((f32[512,256]{1,0:T(8,128)}, f32[512,256]{1,0:T(8,128)}, u32[]{:S(2)}, u32[]{:S(2)}) %collective-permute-start.20) | collective-permute-done | bytes 524320 | tf_op jit(solution)/shard_map/ppermute | solution.py:676
  165.2 2.5 %collective-permute-start.21 = (f32[512,256]{1,0:T(8,128)}, f32[512,256]{1,0:T(8,128)}, u32[]{:S(2)}, u32[]{:S(2)}) collective-permute-start(f32[512,256]{1,0:T(8,128)} %collective-permute-done.20.refs_4_), channel_id=1, source_target_pairs={{0,1},{1,0}} | collective-permute-start | bytes 1572872 | tf_op jit(solution)/shard_map/ppermute | solution.py:676
  167.7 5.8 %all-gather.2.cloned.1.call-done.refs_1_.refs_5_ = f32[512,1280]{1,0:T(8,128)} async-done(((f32[32,1280]{1,0:T(8,128)}), f32[512,1280]{1,0:T(8,128)}) %all-gather.2.cloned.1.call-update) | async-done | bytes 2621456 | tf_op jit(solution)/shard_map/all_gather | solution.py:728
  173.6 1.9 slice.16
  175.4 1.5 collective-permute-start.24
  176.9 2.5 %collective-permute-start.10 = (f32[512,256]{1,0:T(8,128)}, f32[512,256]{1,0:T(8,128)S(1)}, u32[]{:S(2)}, u32[]{:S(2)}) collective-permute-start(f32[512,256]{1,0:T(8,128)} %slice.16), channel_id=1, source_target_pairs={{0,1},{1,0},{4,5},{5,4},{8,9},{9,8},{12,13},{13,12},{16,17},{17,16... | collective-permute-start | bytes 1572872 | tf_op jit(solution)/shard_map/ppermute | solution.py:676
  179.5 1.5 collective-permute-start.13
  180.9 1.5 collective-permute-start.16
  182.4 1.9 collective-permute-start.23
  184.3 0.9 shard_map.40.refs_19_
  185.3 1.3 copy-done.3
  186.6 0.8 copy-done.8
  187.4 5.4 %shard_map.38.refs_14_ = f32[512,512]{1,0:T(8,128)} custom-call(s32[4]{0:T(128)} %pad_add_fusion.refs_0_, f32[512,1280]{1,0:T(8,128)} %all-gather.2.cloned.1.call-done.refs_1_.refs_5_, f32[512,256]{1,0:T(8,128)} %copy-done.8, f32[16,32,1024]{2,1,0:T(8,128)} %copy-done.3, f32[512,256]{1,0:T(8,128)} %collective-permute-done.20.refs_4_, ...), custom_call_target="tpu_custom_call" | custom-call | tf_op jit(solution)/shard_map/pallas_call | solution.py:158
  192.9 5.5 %shard_map.41 = f32[1,512,1,512]{3,2,1,0:T(1,128)} custom-call(s32[4]{0:T(128)} %pad_add_fusion.refs_0_, f32[1,512,1,512]{3,2,1,0:T(1,128)} %refs_1_.7, f32[1,512,1,512]{3,2,1,0:T(1,128)} %copy-done.2, f32[1,512,1,512]{3,2,1,0:T(1,128)} %collective-permute-done.1.refs_1_.refs_3_, f32[1,512,1,512]{3,2,1,0:T(1,128)} %collective-permute-done.5.refs_2_.refs_4_, ...), custom_call_target="tpu_custom_call" | custom-call | tf_op jit(solution)/shard_map/pallas_call | solution.py:158
  (55 shorter events, 2.7 us)
Async XLA Ops:
  6.5 3.7 %collective-permute-start.2 = (f32[1,512,1,512]{3,2,1,0:T(1,128)}, f32[1,512,1,512]{3,2,1,0:T(1,128)S(1)}, u32[]{:S(2)}, u32[]{:S(2)}) collective-permute-start(f32[1,512,1,512]{3,2,1,0:T(1,128)} %refs_6_.1), channel_id=1, source_target_pairs={{2,3},{3,2},{6,7},{7,6},{10,11},{11,10},{14,15},{15,14},{18,19},{1... | collective-permute-start | bytes 3145736 | tf_op jit(solution)/shard_map/ppermute | solution.py:676
  7.3 3.0 %collective-permute-start = (f32[1,512,1,512]{3,2,1,0:T(1,128)}, f32[1,512,1,512]{3,2,1,0:T(1,128)S(1)}, u32[]{:S(2)}, u32[]{:S(2)}) collective-permute-start(f32[1,512,1,512]{3,2,1,0:T(1,128)} %refs_1_.7), channel_id=1, source_target_pairs={{2,3},{3,2},{6,7},{7,6},{10,11},{11,10},{14,15},{15,14},{18,19},{1... | collective-permute-start | bytes 3145736 | tf_op jit(solution)/shard_map/ppermute | solution.py:676
  8.0 15.9 %collective-permute-start.3 = (f32[1,512,1,512]{3,2,1,0:T(1,128)}, f32[1,512,1,512]{3,2,1,0:T(1,128)}, u32[]{:S(2)}, u32[]{:S(2)}) collective-permute-start(f32[1,512,1,512]{3,2,1,0:T(1,128)} %refs_6_.1), channel_id=1, source_target_pairs={{7,5},{2,0},{6,4}} | collective-permute-start | bytes 3145736 | tf_op jit(solution)/shard_map/ppermute | solution.py:676
  10.3 1.0 copy-start.4
  11.3 1.1 copy-start.2
  14.3 29.2 %all-to-all-start = ((f32[16,32,768]{2,1,0:T(8,128)}), f32[16,32,768]{2,1,0:T(8,128)S(1)}, u32[]{:S(2)}, u32[]{:S(2)}) async-start(f32[16,32,768]{2,1,0:T(8,128)} %shard_map.28), calls=%async_computation | async-start | bytes 3145728 | tf_op jit(solution)/shard_map/all_to_all | solution.py:688
  23.0 7.2 %copy-start.1 = (f32[1,512,1,512]{3,2,1,0:T(1,128)S(1)}, f32[1,512,1,512]{3,2,1,0:T(1,128)}, u32[]{:S(2)}) copy-start(f32[1,512,1,512]{3,2,1,0:T(1,128)} %refs_1_.7) | copy-start | bytes 3145732
  23.9 8.8 %collective-permute-start.4 = (f32[1,512,1,512]{3,2,1,0:T(1,128)}, f32[1,512,1,512]{3,2,1,0:T(1,128)S(1)}, u32[]{:S(2)}, u32[]{:S(2)}) collective-permute-start(f32[1,512,1,512]{3,2,1,0:T(1,128)} %collective-permute-done.3.refs_2_), channel_id=1, source_target_pairs={{0,1},{1,0},{4,5},{5,4}} | collective-permute-start | bytes 3145736 | tf_op jit(solution)/shard_map/ppermute | solution.py:676
  30.2 26.4 %collective-permute-start.1 = (f32[1,512,1,512]{3,2,1,0:T(1,128)S(1)}, f32[1,512,1,512]{3,2,1,0:T(1,128)}, u32[]{:S(2)}, u32[]{:S(2)}) collective-permute-start(f32[1,512,1,512]{3,2,1,0:T(1,128)S(1)} %copy-done.1), channel_id=1, source_target_pairs={{10,8},{11,9},{14,12},{15,13},{18,16},{19,17},{22,20},{23,21},{26,... | collective-permute-start | bytes 3145736 | tf_op jit(solution)/shard_map/ppermute | solution.py:676
  32.6 1.0 copy-start.9
  43.6 35.2 %all-to-all-start.1 = ((f32[16,32,768]{2,1,0:T(8,128)}), f32[16,32,768]{2,1,0:T(8,128)}, u32[]{:S(2)}, u32[]{:S(2)}) async-start(f32[16,32,768]{2,1,0:T(8,128)} %get-tuple-element.32), calls=%async_computation.1 | async-start | bytes 3145728 | tf_op jit(solution)/shard_map/all_to_all | solution.py:688
  56.6 10.2 %collective-permute-start.5 = (f32[1,512,1,512]{3,2,1,0:T(1,128)}, f32[1,512,1,512]{3,2,1,0:T(1,128)}, u32[]{:S(2)}, u32[]{:S(2)}) collective-permute-start(f32[1,512,1,512]{3,2,1,0:T(1,128)} %collective-permute-done.1.refs_1_.refs_3_), channel_id=1, source_target_pairs={{4,5},{5,4},{8,9},{9,8},{12,13},{13,12},{16,17},{17,16},{20,21},{2... | collective-permute-start | bytes 3145736 | tf_op jit(solution)/shard_map/ppermute | solution.py:676
  58.3 26.1 %collective-permute-start.8 = (f32[512,512]{1,0:T(8,128)}, f32[512,512]{1,0:T(8,128)S(1)}, u32[]{:S(2)}, u32[]{:S(2)}) collective-permute-start(f32[512,512]{1,0:T(8,128)} %get-tuple-element.30.refs_5_.refs_7_), channel_id=1, source_target_pairs={{6,2}} | collective-permute-start | bytes 3145736 | tf_op jit(solution)/shard_map/ppermute | solution.py:676
  59.1 7.7 %copy-start.14 = (f32[32,768]{1,0:T(8,128)}, f32[32,768]{1,0:T(8,128)S(1)}, u32[]{:S(2)}) copy-start(f32[32,768]{1,0:T(8,128)S(1)} %reduce_sum.9.refs_4_) | copy-start | bytes 294916
  59.1 7.7 %collective-permute-start.6 = (f32[32,768]{1,0:T(8,128)S(1)}, f32[32,768]{1,0:T(8,128)S(1)}, u32[]{:S(2)}, u32[]{:S(2)}) collective-permute-start(f32[32,768]{1,0:T(8,128)S(1)} %reduce_sum.9.refs_4_), channel_id=1, source_target_pairs={{0,16},{16,0},{1,17},{17,1},{2,18},{18,2},{3,19},{19,3},{4,20},{20... | collective-permute-start | bytes 294920 | tf_op jit(solution)/shard_map/ppermute | solution.py:684
  66.8 0.7 copy-start.16
  78.8 31.1 %all-to-all-start.2 = ((f32[16,32,1024]{2,1,0:T(8,128)}), f32[16,32,1024]{2,1,0:T(8,128)S(1)}, u32[]{:S(2)}, u32[]{:S(2)}) async-start(f32[16,32,1024]{2,1,0:T(8,128)} %shard_map.31), calls=%async_computation.2 | async-start | bytes 4194304 | tf_op jit(solution)/shard_map/all_to_all | solution.py:688
  84.3 89.2 %all-gather.2.cloned.1.call-start = ((), (), s32[]{:S(2)}) async-start(), calls=%async_computation.4 | async-start | bytes 2785280 | tf_op jit(solution)/shard_map/all_gather | solution.py:728
  84.4 27.6 %copy-start.5 = (f32[512,512]{1,0:T(8,128)}, f32[512,512]{1,0:T(8,128)S(1)}, u32[]{:S(2)}) copy-start(f32[512,512]{1,0:T(8,128)S(1)} %collective-permute-done.8.refs_7_.refs_4_.refs_3_) | copy-start | bytes 3145732
  84.4 7.7 %collective-permute-start.9 = (f32[512,512]{1,0:T(8,128)S(1)}, f32[512,512]{1,0:T(8,128)}, u32[]{:S(2)}, u32[]{:S(2)}) collective-permute-start(f32[512,512]{1,0:T(8,128)S(1)} %collective-permute-done.8.refs_7_.refs_4_.refs_3_), channel_id=1, source_target_pairs={{2,3}} | collective-permute-start | bytes 3145736 | tf_op jit(solution)/shard_map/ppermute | solution.py:676
  87.8 3.5 %collective-permute-start.7 = (f32[32,1280]{1,0:T(8,128)S(1)}, f32[32,1280]{1,0:T(8,128)S(1)}, u32[]{:S(2)}, u32[]{:S(2)}) collective-permute-start(f32[32,1280]{1,0:T(8,128)S(1)} %pad_maximum_fusion), channel_id=1, source_target_pairs={{0,16},{1,17},{2,18},{3,19},{4,20},{5,21},{6,22},{7,23},{8,24},{9,... | collective-permute-start | bytes 491528 | tf_op jit(solution)/shard_map/ppermute | solution.py:726
  109.9 1.3 copy-start
  110.0 2.0 copy-start.6
  110.0 15.7 %collective-permute-start.18 = (f32[16,32,256]{2,1,0:T(8,128)S(1)}, f32[16,32,256]{2,1,0:T(8,128)S(1)}, u32[]{:S(2)}, u32[]{:S(2)}) collective-permute-start(f32[16,32,256]{2,1,0:T(8,128)S(1)} %slice.15.refs_2_), channel_id=1, source_target_pairs={{2,3},{3,2}} | collective-permute-start | bytes 1572872 | tf_op jit(solution)/shard_map/ppermute | solution.py:676
  112.0 15.3 %collective-permute-start.17 = (f32[512,256]{1,0:T(8,128)}, f32[512,256]{1,0:T(8,128)S(1)}, u32[]{:S(2)}, u32[]{:S(2)}) collective-permute-start(f32[512,256]{1,0:T(8,128)} %shard_map.32.refs_2_), channel_id=1, source_target_pairs={{6,2},{7,3}} | collective-permute-start | bytes 1572872 | tf_op jit(solution)/shard_map/ppermute | solution.py:676
  115.1 7.4 %collective-permute-start.11 = (f32[32,1024]{1,0:T(8,128)}, f32[32,1024]{1,0:T(8,128)S(1)}, u32[]{:S(2)}, u32[]{:S(2)}) collective-permute-start(f32[32,1024]{1,0:T(8,128)} %shard_map.33.refs_0_), channel_id=1, source_target_pairs={{16,0},{17,1},{18,2},{19,3},{20,4},{21,5},{22,6},{23,7},{24,8},{25... | collective-permute-start | bytes 393224 | tf_op jit(solution)/shard_map/ppermute | solution.py:738
  122.5 0.6 copy-start.15
  125.7 0.8 copy-start.12
  127.2 7.3 %copy-start.7 = (f32[512,256]{1,0:T(8,128)S(1)}, f32[512,256]{1,0:T(8,128)}, u32[]{:S(2)}) copy-start(f32[512,256]{1,0:T(8,128)} %shard_map.32.refs_2_) | copy-start | bytes 1572868
  127.3 1.6 copy-start.11
  127.3 8.0 %collective-permute-start.19 = (f32[512,256]{1,0:T(8,128)S(1)}, f32[512,256]{1,0:T(8,128)}, u32[]{:S(2)}, u32[]{:S(2)}) collective-permute-start(f32[512,256]{1,0:T(8,128)S(1)} %collective-permute-done.17.refs_2_), channel_id=1, source_target_pairs={{2,3},{3,2}} | collective-permute-start | bytes 1572872 | tf_op jit(solution)/shard_map/ppermute | solution.py:676
  128.9 56.4 %all-to-all-start.3 = ((f32[16,32,1024]{2,1,0:T(8,128)}), f32[16,32,1024]{2,1,0:T(8,128)S(1)}, u32[]{:S(2)}, u32[]{:S(2)}) async-start(f32[16,32,1024]{2,1,0:T(8,128)} %shard_map.34), calls=%async_computation.3 | async-start | bytes 4194304 | tf_op jit(solution)/shard_map/all_to_all | solution.py:688
  134.6 3.4 %collective-permute-start.14 = (f32[512,256]{1,0:T(8,128)S(1)}, f32[512,256]{1,0:T(8,128)S(1)}, u32[]{:S(2)}, u32[]{:S(2)}) collective-permute-start(f32[512,256]{1,0:T(8,128)S(1)} %copy-done.7), channel_id=1, source_target_pairs={{6,7},{7,6}} | collective-permute-start | bytes 1572872 | tf_op jit(solution)/shard_map/ppermute | solution.py:676
  136.0 29.2 %collective-permute-start.20 = (f32[512,256]{1,0:T(8,128)}, f32[512,256]{1,0:T(8,128)}, u32[]{:S(2)}, u32[]{:S(2)}) collective-permute-start(f32[512,256]{1,0:T(8,128)} %shard_map.37.refs_2_), channel_id=1, source_target_pairs={{2,0},{3,1}} | collective-permute-start | bytes 1572872 | tf_op jit(solution)/shard_map/ppermute | solution.py:676
  137.3 38.1 %collective-permute-start.12 = (f32[512,256]{1,0:T(8,128)S(1)}, f32[512,256]{1,0:T(8,128)S(1)}, u32[]{:S(2)}, u32[]{:S(2)}) collective-permute-start(f32[512,256]{1,0:T(8,128)S(1)} %copy-done.7), channel_id=1, source_target_pairs={{6,4},{7,5}} | collective-permute-start | bytes 1572872 | tf_op jit(solution)/shard_map/ppermute | solution.py:676
  138.0 0.8 copy-start.13
  139.6 37.3 %collective-permute-start.15 = (f32[512,256]{1,0:T(8,128)}, f32[512,256]{1,0:T(8,128)}, u32[]{:S(2)}, u32[]{:S(2)}) collective-permute-start(f32[512,256]{1,0:T(8,128)} %get-tuple-element.43), channel_id=1, source_target_pairs={{6,4},{7,5}} | collective-permute-start | bytes 1572872 | tf_op jit(solution)/shard_map/ppermute | solution.py:676
  141.8 37.7 %collective-permute-start.25 = (f32[512,256]{1,0:T(8,128)}, f32[512,256]{1,0:T(8,128)}, u32[]{:S(2)}, u32[]{:S(2)}) collective-permute-start(f32[512,256]{1,0:T(8,128)} %shard_map.39.refs_2_), channel_id=1, source_target_pairs={{3,2}} | collective-permute-start | bytes 1572872 | tf_op jit(solution)/shard_map/ppermute | solution.py:676
  143.3 37.7 %collective-permute-start.22 = (f32[512,256]{1,0:T(8,128)}, f32[512,256]{1,0:T(8,128)}, u32[]{:S(2)}, u32[]{:S(2)}) collective-permute-start(f32[512,256]{1,0:T(8,128)} %shard_map.39.refs_2_), channel_id=1, source_target_pairs={{2,0},{3,1}} | collective-permute-start | bytes 1572872 | tf_op jit(solution)/shard_map/ppermute | solution.py:676
  165.2 17.2 %collective-permute-start.21 = (f32[512,256]{1,0:T(8,128)}, f32[512,256]{1,0:T(8,128)}, u32[]{:S(2)}, u32[]{:S(2)}) collective-permute-start(f32[512,256]{1,0:T(8,128)} %collective-permute-done.20.refs_4_), channel_id=1, source_target_pairs={{0,1},{1,0}} | collective-permute-start | bytes 1572872 | tf_op jit(solution)/shard_map/ppermute | solution.py:676
  175.4 9.8 %copy-start.10 = (f32[512,256]{1,0:T(8,128)}, f32[512,256]{1,0:T(8,128)S(1)}, u32[]{:S(2)}) copy-start(f32[512,256]{1,0:T(8,128)S(1)} %collective-permute-done.12.refs_10_) | copy-start | bytes 1572868
  175.4 17.4 %collective-permute-start.24 = (f32[512,256]{1,0:T(8,128)}, f32[512,256]{1,0:T(8,128)}, u32[]{:S(2)}, u32[]{:S(2)}) collective-permute-start(f32[512,256]{1,0:T(8,128)} %get-tuple-element.47.refs_17_), channel_id=1, source_target_pairs={{7,6}} | collective-permute-start | bytes 1572872 | tf_op jit(solution)/shard_map/ppermute | solution.py:676
  176.9 8.4 %collective-permute-start.10 = (f32[512,256]{1,0:T(8,128)}, f32[512,256]{1,0:T(8,128)S(1)}, u32[]{:S(2)}, u32[]{:S(2)}) collective-permute-start(f32[512,256]{1,0:T(8,128)} %slice.16), channel_id=1, source_target_pairs={{0,1},{1,0},{4,5},{5,4},{8,9},{9,8},{12,13},{13,12},{16,17},{17,16... | collective-permute-start | bytes 1572872 | tf_op jit(solution)/shard_map/ppermute | solution.py:676
  179.5 13.4 %collective-permute-start.13 = (f32[512,256]{1,0:T(8,128)S(1)}, f32[512,256]{1,0:T(8,128)}, u32[]{:S(2)}, u32[]{:S(2)}) collective-permute-start(f32[512,256]{1,0:T(8,128)S(1)} %collective-permute-done.12.refs_10_), channel_id=1, source_target_pairs={{4,5},{5,4}} | collective-permute-start | bytes 1572872 | tf_op jit(solution)/shard_map/ppermute | solution.py:676
  180.9 11.9 %collective-permute-start.16 = (f32[512,256]{1,0:T(8,128)}, f32[512,256]{1,0:T(8,128)}, u32[]{:S(2)}, u32[]{:S(2)}) collective-permute-start(f32[512,256]{1,0:T(8,128)} %collective-permute-done.15.refs_12_), channel_id=1, source_target_pairs={{4,5},{5,4}} | collective-permute-start | bytes 1572872 | tf_op jit(solution)/shard_map/ppermute | solution.py:676
  182.4 10.5 %collective-permute-start.23 = (f32[512,256]{1,0:T(8,128)}, f32[512,256]{1,0:T(8,128)}, u32[]{:S(2)}, u32[]{:S(2)}) collective-permute-start(f32[512,256]{1,0:T(8,128)} %collective-permute-done.22.refs_15_), channel_id=1, source_target_pairs={{0,1},{1,0}} | collective-permute-start | bytes 1572872 | tf_op jit(solution)/shard_map/ppermute | solution.py:676
  185.3 1.4 copy-start.3
  186.6 0.8 copy-start.8
Sparse Core Ops, SparseCore 0:
  110.0 63.4 all-gather.1
